TPU v7x, 32 devices: a whole 2x2x4 slice. The times are simulated.
32 devices in a mesh: row: 8 (over z, x), col: 4 (over y, core).
Axes of the slice: x: 2, y: 2, z: 4, core: 2. Of those that a mesh axis runs over, the one named last changes fastest.
Arguments:
- object_field: float32 [2, 4096, 1536], P(None, 'row', 'col'), may hold values from -6 to 6
- probe_field: float32 [2, 256, 256], replicated, may hold values from -6 to 6
- amplitudes: bfloat16 [2, 384, 256, 256], P(None, ('row', 'col')), may hold values from 0.29882812 to 3
- positions: int32 [2, 2, 384], P(None, None, ('row', 'col')), may hold values from 0 to 511, as said below
- live_counts: int32 [2, 4, 8], P(None, 'col', 'row'), may hold values from 1 to 12, 24 in all within a row
Outputs:
- object_out: float32 [2, 4096, 1536], P(None, 'row', 'col')
- probe_out: float32 [2, 256, 256], replicated
Inputs may be any that keep to these rules, and one draw needn't show every extreme that they name: `positions`: every offset is below 512 for rows and below 384 for columns; in the last block row the row offset is at most 256, in the last block column the column offset at most 128, so every patch lies inside the object. The live frames of a device are its first slots. For every iteration t and block column c, the 8 counts live_counts[t, c, :] of that block column's devices sum to 24, and one of them is 12; no such sum holds over the devices of a block row.
All inputs are finite; a program needn't handle non-finite values.
Results may differ from a plain program's by a relative error of at most 0.0019.
Values may be sent and summed in bfloat16 or wider, within the bound.
A program may use at most 128 MiB of HBM per device.

v0:
```python
import functools
import math

import jax
import jax.numpy as jnp
import ml_dtypes
import numpy as np
from jax import lax
from jax.experimental import pallas as pl
from jax.experimental.pallas import tpu as pltpu
from jax.sharding import PartitionSpec as P

ITERS = 2


FLOOR = 0.3
ALPHA = 0.5
LANES = 128
SUBLANES = 8
MESH = pl.DeviceIdType.MESH


def passed_along(value, axis, steps):
    count = lax.axis_size(axis)
    first, last = (max(0, -steps), min(count, count - steps))
    return lax.ppermute(value, axis, [(source, source + steps) for source in range(first, last)])


def chirp_blocks(frame_size):
    offset = np.arange(frame_size, dtype=np.int32)
    differ = offset[:, None] - offset[None, :]
    phase = np.pi * (differ * differ % (2 * frame_size)).astype(np.float64) / frame_size
    scale = 1.0 / math.sqrt(frame_size)
    real, imag = (np.cos(phase) * scale, np.sin(phase) * scale)
    forward = np.block([[real, -imag], [imag, real]]).astype(ml_dtypes.bfloat16)
    return jnp.asarray(forward), jnp.asarray(forward.T.copy())


def frames_kernel(
    positions, live, extended, probe, amplitudes, left_table, right_table, gathered, sums
):
    size = probe.shape[-1]
    halves = size // LANES
    gathered[...] = jnp.zeros_like(gathered)
    sums[...] = jnp.zeros_like(sums)
    groups = size // SUBLANES
    lane = lax.broadcasted_iota(jnp.int32, (groups + 1, SUBLANES, LANES), 2)
    sublane = lax.broadcasted_iota(jnp.int32, (groups, SUBLANES, LANES), 1)

    def dot(a, b):
        return jnp.dot(a, b, preferred_element_type=jnp.float32)

    def one_frame(slot, weight):
        top = positions[0, slot]
        left = positions[1, slot]
        block = left // LANES
        shift = left - block * LANES
        row_block = top // SUBLANES
        row_shift = top - row_block * SUBLANES
        rows = pl.ds(row_block, groups + 1)

        def columns(part):
            return pl.ds(pl.multiple_of((block + part) * LANES, LANES), LANES)

        patch = []
        back_shift = lax.rem(LANES - shift, LANES)
        back_row_shift = lax.rem(SUBLANES - row_shift, SUBLANES)
        keep = lane < LANES - shift
        keep_rows = sublane < SUBLANES - row_shift
        for comp in range(2):
            turned = [
                pltpu.roll(extended[comp, rows, :, columns(part)], back_shift, 2)
                for part in range(halves + 1)
            ]
            picked = []
            for part in range(halves):
                tall = pltpu.roll(
                    jnp.where(keep, turned[part], turned[part + 1]), back_row_shift, 1
                )
                picked.append(
                    jnp.where(keep_rows, tall[:groups], tall[1:]).reshape(size, LANES)
                )
            patch.append(
                jnp.concatenate(picked, axis=1).astype(jnp.bfloat16).astype(jnp.float32)
            )
        patch_real, patch_imag = patch
        probe_real, probe_imag = probe[0], probe[1]
        wave = jnp.concatenate(
            [
                probe_real * patch_real - probe_imag * patch_imag,
                probe_real * patch_imag + probe_imag * patch_real,
            ],
            axis=0,
        ).astype(jnp.bfloat16)
        near = dot(left_table[...], wave).astype(jnp.bfloat16)
        far = dot(jnp.concatenate([near[:size], near[size:]], axis=1), right_table[...])
        far_real, far_imag = far[:, :size], far[:, size:]
        power = far_real * far_real + far_imag * far_imag
        factor = 1.0 - amplitudes[slot].astype(jnp.float32) * lax.rsqrt(
            jnp.maximum(power, FLOOR * FLOOR)
        )
        misfit = jnp.concatenate([far_real * factor, far_imag * factor], axis=0).astype(
            jnp.bfloat16
        )
        back = dot(right_table[...], misfit).astype(jnp.bfloat16)
        update = dot(jnp.concatenate([back[:size], back[size:]], axis=1), left_table[...])
        update_real, update_imag = update[:, :size] * weight, update[:, size:] * weight
        terms = (
            patch_real * update_real + patch_imag * update_imag,
            patch_real * update_imag - patch_imag * update_real,
            (patch_real * patch_real + patch_imag * patch_imag) * weight,
        )
        for comp, term in enumerate(terms):
            for half in range(halves):
                sums[comp * halves + half] += term[:, half * LANES : (half + 1) * LANES]
        grads = (
            probe_real * update_real + probe_imag * update_imag,
            probe_real * update_imag - probe_imag * update_real,
        )
        moved = lane >= shift
        moved_rows = sublane >= row_shift
        for comp, grad in enumerate(grads):
            grad = grad.astype(jnp.bfloat16).astype(jnp.float32)
            turned = []
            for half in range(halves):
                tall = pltpu.roll(
                    grad[:, half * LANES : (half + 1) * LANES].reshape(groups, SUBLANES, LANES),
                    row_shift,
                    1,
                )
                tall = jnp.concatenate(
                    [
                        jnp.where(moved_rows[:1], tall[:1], 0.0),
                        jnp.where(moved_rows[1:], tall[1:], tall[:-1]),
                        jnp.where(moved_rows[:1], 0.0, tall[-1:]),
                    ],
                    axis=0,
                )
                turned.append(pltpu.roll(tall, shift, 2))
            nothing = jnp.zeros_like(turned[0])
            before = [nothing] + turned
            after = turned + [nothing]
            for part in range(halves + 1):
                gathered[comp, rows, :, columns(part)] += jnp.where(
                    moved, after[part], before[part]
                )

    count = live[0]

    def pair(index, carry):
        one_frame(2 * index, jnp.float32(1.0))
        one_frame(2 * index + 1, (2 * index + 1 < count).astype(jnp.float32))
        return carry

    lax.fori_loop(0, (count + 1) // 2, pair, 0)


def frame_sums(extended, probe_field, amplitudes, positions, live, tables):
    size = probe_field.shape[-1]
    slots = amplitudes.shape[0]
    vmem = pl.BlockSpec(memory_space=pltpu.VMEM)
    smem = pl.BlockSpec(memory_space=pltpu.SMEM)
    planes, tall, width = extended.shape
    extended = extended.reshape(planes, tall // SUBLANES, SUBLANES, width)
    gathered, sums = pl.pallas_call(
        frames_kernel,
        out_shape=(
            jax.ShapeDtypeStruct(extended.shape, jnp.float32),
            jax.ShapeDtypeStruct((3 * size // LANES, size, LANES), jnp.float32),
        ),
        in_specs=[smem, smem] + [vmem] * 5,
        out_specs=(vmem, vmem),
        compiler_params=pltpu.CompilerParams(vmem_limit_bytes=48 * 1024 * 1024),
        cost_estimate=pl.CostEstimate(
            flops=slots * 32 * size**3,
            bytes_accessed=12 * 1024 * 1024,
            transcendentals=slots * size * size,
        ),
        name="frames",
    )(positions, live, extended, probe_field, amplitudes, *tables)
    return gathered.reshape(planes, tall, width), sums


def probe_kernel(
    n_row,
    n_col,
    sums,
    probe,
    out,
    wide,
    got_col,
    own_rows,
    got_row,
    piece,
    steps,
    joined,
    got_steps,
    col_send,
    col_recv,
    row_send,
    row_recv,
    back_row_send,
    back_row_recv,
    back_col_send,
    back_col_recv,
):
    row, col = lax.axis_index("row"), lax.axis_index("col")
    planes, size, _ = sums.shape
    chunk = size // n_col
    part = chunk // n_row
    comps = planes * 2 // 3

    def along_col(step):
        return (row, lax.rem(col + step, n_col))

    def along_row(step):
        return (lax.rem(row + step, n_row), col)

    barrier = pltpu.get_barrier_semaphore()
    for step in range(1, n_col):
        pl.semaphore_signal(barrier, inc=1, device_id=along_col(step), device_id_type=MESH)
    for step in range(1, n_row):
        pl.semaphore_signal(barrier, inc=1, device_id=along_row(step), device_id_type=MESH)
    wide[...] = sums[...].astype(jnp.bfloat16)
    pl.semaphore_wait(barrier, n_col + n_row - 2)

    def remote(source, target, send, recv, device):
        copy = pltpu.make_async_remote_copy(
            src_ref=source,
            dst_ref=target,
            send_sem=send,
            recv_sem=recv,
            device_id=device,
            device_id_type=MESH,
        )
        copy.start()
        return copy

    def rows_of(index, length):
        return pl.ds(pl.multiple_of(index * length, length), length)

    first = []
    for step in range(1, n_col):
        their = lax.rem(col + step, n_col)
        first.append(
            remote(
                wide.at[:, rows_of(their, chunk), :],
                got_col.at[step - 1],
                col_send.at[step - 1],
                col_recv.at[step - 1],
                along_col(step),
            )
        )
    total = sums[:, rows_of(col, chunk), :]
    for step, copy in enumerate(first):
        copy.wait_recv()
        total = total + got_col[step].astype(jnp.float32)
    for index in range(n_row):
        own_rows[index] = total[:, index * part : (index + 1) * part, :]
    second = []
    for step in range(1, n_row):
        their = lax.rem(row + step, n_row)
        second.append(
            remote(
                own_rows.at[their],
                got_row.at[step - 1],
                row_send.at[step - 1],
                row_recv.at[step - 1],
                along_row(step),
            )
        )
    total = own_rows[row]
    for step, copy in enumerate(second):
        copy.wait_recv()
        total = total + got_row[step]
    halves = planes // 3
    weight = total[2 * halves :] + 1.0
    piece[...] = jnp.concatenate(
        [total[:halves] / weight, total[halves : 2 * halves] / weight], axis=0
    )
    third = [
        remote(
            piece,
            steps.at[row],
            back_row_send.at[step - 1],
            back_row_recv.at[step - 1],
            along_row(step),
        )
        for step in range(1, n_row)
    ]
    steps[row] = piece[...]
    for copy in third:
        copy.wait_recv()
    joined[...] = jnp.concatenate([steps[index] for index in range(n_row)], axis=1)
    fourth = [
        remote(
            joined,
            got_steps.at[col],
            back_col_send.at[step - 1],
            back_col_recv.at[step - 1],
            along_col(step),
        )
        for step in range(1, n_col)
    ]
    got_steps[col] = joined[...]
    for copy in fourth:
        copy.wait_recv()
    for index in range(n_col):
        rows = slice(index * chunk, (index + 1) * chunk)
        for plane in range(comps):
            comp, half = divmod(plane, halves)
            lanes = slice(half * LANES, (half + 1) * LANES)
            out[comp, rows, lanes] = probe[comp, rows, lanes] - got_steps[index, plane]
    for copy in first + second + third + fourth:
        copy.wait_send()


def next_probe(sums, probe_field):
    n_row, n_col = lax.axis_size("row"), lax.axis_size("col")
    planes, size, _ = sums.shape
    chunk = size // n_col
    part = chunk // n_row
    comps = planes * 2 // 3
    vmem = pl.BlockSpec(memory_space=pltpu.VMEM)
    dma = pltpu.SemaphoreType.DMA
    return pl.pallas_call(
        functools.partial(probe_kernel, n_row, n_col),
        out_shape=jax.ShapeDtypeStruct(probe_field.shape, jnp.float32),
        in_specs=[vmem, vmem],
        out_specs=vmem,
        scratch_shapes=[
            pltpu.VMEM(sums.shape, jnp.bfloat16),
            pltpu.VMEM((n_col - 1, planes, chunk, LANES), jnp.bfloat16),
            pltpu.VMEM((n_row, planes, part, LANES), jnp.float32),
            pltpu.VMEM((n_row - 1, planes, part, LANES), jnp.float32),
            pltpu.VMEM((comps, part, LANES), jnp.float32),
            pltpu.VMEM((n_row, comps, part, LANES), jnp.float32),
            pltpu.VMEM((comps, chunk, LANES), jnp.float32),
            pltpu.VMEM((n_col, comps, chunk, LANES), jnp.float32),
            dma((n_col - 1,)),
            dma((n_col - 1,)),
            dma((n_row - 1,)),
            dma((n_row - 1,)),
            dma((n_row - 1,)),
            dma((n_row - 1,)),
            dma((n_col - 1,)),
            dma((n_col - 1,)),
        ],
        compiler_params=pltpu.CompilerParams(
            collective_id=0, has_side_effects=True, vmem_limit_bytes=32 * 1024 * 1024
        ),
        cost_estimate=pl.CostEstimate(
            flops=planes * size * LANES * 4, bytes_accessed=4 * 1024 * 1024, transcendentals=0
        ),
        name="probe_sum",
    )(sums, probe_field)


def extend_block(object_field, frame_size):
    below = passed_along(object_field[:, :frame_size, :].astype(jnp.bfloat16), "row", -1)
    taller = jnp.concatenate([object_field[:, :, :frame_size].astype(jnp.bfloat16), below[:, :, :frame_size]], axis=1)
    beside = passed_along(taller, "col", -1).astype(jnp.float32)
    own = jnp.concatenate([object_field, below.astype(jnp.float32)], axis=1)
    return jnp.concatenate([own, beside], axis=2)


def fold_rims(gathered, block_rows, block_columns):
    from_left = passed_along(gathered[:, :, block_columns:].astype(jnp.bfloat16), "col", 1).astype(
        jnp.float32
    )
    narrow = gathered[:, :, :block_columns]
    narrow = narrow.at[:, :, : from_left.shape[2]].add(from_left)
    from_above = passed_along(narrow[:, block_rows:, :].astype(jnp.bfloat16), "row", 1).astype(
        jnp.float32
    )
    return narrow[:, :block_rows, :].at[:, : from_above.shape[1], :].add(from_above)


def local(object_field, probe_field, amplitudes, positions, live_counts):
    frame_size = probe_field.shape[-1]
    block_rows, block_columns = (object_field.shape[1], object_field.shape[2])
    tables = chirp_blocks(frame_size)
    for iteration in range(ITERS):
        extended = extend_block(object_field, frame_size)
        gathered, sums = frame_sums(
            extended,
            probe_field,
            amplitudes[iteration],
            positions[iteration],
            live_counts[iteration, 0],
            tables,
        )
        object_sum = fold_rims(gathered, block_rows, block_columns)
        step_size = ALPHA / (
            jnp.max(probe_field[0] * probe_field[0] + probe_field[1] * probe_field[1]) + 1e-06
        )
        object_field = object_field - step_size * object_sum
        probe_field = next_probe(sums, probe_field)
    return (object_field, probe_field)


def solution(mesh):
    placed = (
        P(None, "row", "col"),
        P(),
        P(None, ("row", "col"), None, None),
        P(None, None, ("row", "col")),
        P(None, "col", "row"),
    )
    return jax.shard_map(
        local, mesh=mesh, in_specs=placed, out_specs=(P(None, "row", "col"), P()), check_vma=False
    )
```

profile of v0, /device:TPU:25, one launch (start us, length us, event | category | flops | bytes accessed | tf_op | source)
XLA Modules:
  0.0 208.4 jit_solution(7164656649502506541)
XLA Ops:
  0.6 1.5 convert.20
  2.2 3.3 %collective-permute-start = (bf16[2,256,384]{2,1,0:T(8,128)(2,1)S(1)}, bf16[2,256,384]{2,1,0:T(8,128)(2,1)S(1)}, u32[]{:S(2)}, u32[]{:S(2)}) collective-permute-start(bf16[2,256,384]{2,1,0:T(8,128)(2,1)S(1)} %slice.212), channel_id=1, source_target_pairs={{4,0},{8,4},{12,8},{16,12},{20,16},{24,20},{28,24},{5,1},{9,5},{13... | collective-permute-start | bytes 1179656 | tf_op jit(solution)/shard_map/ppermute | solution.py:26
  5.5 8.8 %collective-permute-done = bf16[2,256,384]{2,1,0:T(8,128)(2,1)S(1)} collective-permute-done((bf16[2,256,384]{2,1,0:T(8,128)(2,1)S(1)}, bf16[2,256,384]{2,1,0:T(8,128)(2,1)S(1)}, u32[]{:S(2)}, u32[]{:S(2)}) %collective-permute-start) | collective-permute-done | bytes 393248 | tf_op jit(solution)/shard_map/ppermute | solution.py:26
  14.4 3.5 %collective-permute-start.1 = (bf16[2,768,256]{2,1,0:T(8,128)(2,1)S(1)}, bf16[2,768,256]{2,1,0:T(8,128)(2,1)S(1)}, u32[]{:S(2)}, u32[]{:S(2)}) collective-permute-start(bf16[2,768,256]{2,1,0:T(8,128)(2,1)S(1)} %pad_maximum_fusion), channel_id=1, source_target_pairs={{1,0},{2,1},{3,2},{5,4},{6,5},{7,6},{9,8},{10,9},{11,10},{13,12},{... | collective-permute-start | bytes 2359304 | tf_op jit(solution)/shard_map/ppermute | solution.py:26
  18.9 9.8 %collective-permute-done.1 = bf16[2,768,256]{2,1,0:T(8,128)(2,1)S(1)} collective-permute-done((bf16[2,768,256]{2,1,0:T(8,128)(2,1)S(1)}, bf16[2,768,256]{2,1,0:T(8,128)(2,1)S(1)}, u32[]{:S(2)}, u32[]{:S(2)}) %collective-permute-start.1) | collective-permute-done | bytes 786464 | tf_op jit(solution)/shard_map/ppermute | solution.py:26
  28.9 2.1 %maximum_bitcast_fusion.extended = f32[2,96,8,640]{3,2,1,0:T(8,128)} fusion(f32[2,768,256]{2,1,0:T(8,128)S(1)} %convert_element_type.33, f32[2,256,384]{2,1,0:T(8,128)S(1)} %convert_element_type.32, f32[2,512,384]{2,1,0:T(8,128)S(1)} %copy-done.7), kind=kLoop, calls=%fused_computation | loop fusion | flops 1966080 | bytes 7864320 | tf_op jit(solution)/shard_map/reshape | solution.py:164
  31.0 11.3 %frames.2 = (f32[2,96,8,640]{3,2,1,0:T(8,128)}, f32[6,256,128]{2,1,0:T(8,128)S(1)}) custom-call(s32[2,12]{1,0:T(2,128)S(1)} %get-tuple-element.63.positions, s32[1]{0:T(128)} %bitcast.1.live, f32[2,96,8,640]{3,2,1,0:T(8,128)} %maximum_bitcast_fusion.extended, f32[2,256,256]{2,1,0:T(8,128)S(1)} %copy-done, ...), custom_call_target="tpu_custom_call" | custom-call | flops 6442450944 | bytes 12582912 | tf_op jit(solution)/shard_map/frames/pallas_call | solution.py:165
  42.3 1.5 slice.255
  43.8 1.9 collective-permute-start.2
  45.7 1.8 slice.215
  47.5 7.1 %collective-permute-done.2 = bf16[2,768,256]{2,1,0:T(8,128)(2,1)S(1)} collective-permute-done((bf16[2,768,256]{2,1,0:T(8,128)(2,1)S(1)}, bf16[2,768,256]{2,1,0:T(8,128)(2,1)S(1)}, u32[]{:S(2)}, u32[]{:S(2)}) %collective-permute-start.2) | collective-permute-done | bytes 786464 | tf_op jit(solution)/shard_map/ppermute | solution.py:26
  54.6 1.6 fusion.1
  56.2 1.4 copy-done.9
  57.7 1.9 collective-permute-start.3
  61.0 1.5 slice.218
  62.5 4.7 %collective-permute-done.3 = bf16[2,256,384]{2,1,0:T(8,128)(2,1)} collective-permute-done((bf16[2,256,384]{2,1,0:T(8,128)(2,1)S(1)}, bf16[2,256,384]{2,1,0:T(8,128)(2,1)}, u32[]{:S(2)}, u32[]{:S(2)}) %collective-permute-start.3) | collective-permute-done | bytes 393248 | tf_op jit(solution)/shard_map/ppermute | solution.py:26
  68.8 1.9 collective-permute-start.4
  70.8 6.5 %collective-permute-done.4 = bf16[2,256,384]{2,1,0:T(8,128)(2,1)S(1)} collective-permute-done((bf16[2,256,384]{2,1,0:T(8,128)(2,1)S(1)}, bf16[2,256,384]{2,1,0:T(8,128)(2,1)S(1)}, u32[]{:S(2)}, u32[]{:S(2)}) %collective-permute-start.4) | collective-permute-done | bytes 393248 | tf_op jit(solution)/shard_map/ppermute | solution.py:26
  77.4 1.9 collective-permute-start.5
  79.4 49.8 %probe_sum.2.probe = f32[2,256,256]{2,1,0:T(8,128)S(1)} custom-call(f32[6,256,128]{2,1,0:T(8,128)S(1)} %get-tuple-element.55.sums, f32[2,256,256]{2,1,0:T(8,128)S(1)} %copy-done), custom_call_target="tpu_custom_call" | custom-call | flops 786432 | bytes 4194304 | tf_op jit(solution)/shard_map/probe_sum/pallas_call | solution.py:326
  129.4 2.1 %maximum_bitcast_fusion.1.extended = f32[2,96,8,640]{3,2,1,0:T(8,128)} fusion(f32[2,768,256]{2,1,0:T(8,128)S(1)} %convert_element_type.37, f32[2,256,384]{2,1,0:T(8,128)S(1)} %convert_element_type.36, f32[2,512,384]{2,1,0:T(8,128)S(1)} %get-tuple-element.59), kind=kLoop, calls=%fused_computation.1 | loop fusion | flops 1966080 | bytes 7864320 | tf_op jit(solution)/shard_map/reshape | solution.py:164
  131.5 24.1 %frames.3 = (f32[2,96,8,640]{3,2,1,0:T(8,128)}, f32[6,256,128]{2,1,0:T(8,128)S(1)}) custom-call(s32[2,12]{1,0:T(2,128)S(1)} %get-tuple-element.62.positions, s32[1]{0:T(128)} %bitcast.6.live, f32[2,96,8,640]{3,2,1,0:T(8,128)} %maximum_bitcast_fusion.1.extended, f32[2,256,256]{2,1,0:T(8,128)S(1)} %probe_sum.2.probe, ...), custom_call_target="tpu_custom_call" | custom-call | flops 6442450944 | bytes 12582912 | tf_op jit(solution)/shard_map/frames/pallas_call | solution.py:165
  155.7 1.5 slice.254
  157.2 1.9 collective-permute-start.6
  159.1 1.8 slice.224
  160.9 7.1 %collective-permute-done.6 = bf16[2,768,256]{2,1,0:T(8,128)(2,1)S(1)} collective-permute-done((bf16[2,768,256]{2,1,0:T(8,128)(2,1)S(1)}, bf16[2,768,256]{2,1,0:T(8,128)(2,1)S(1)}, u32[]{:S(2)}, u32[]{:S(2)}) %collective-permute-start.6) | collective-permute-done | bytes 786464 | tf_op jit(solution)/shard_map/ppermute | solution.py:26
  168.0 1.6 fusion
  169.6 1.4 copy-done.10
  171.8 1.9 collective-permute-start.7
  175.2 27.8 %probe_sum.3 = f32[2,256,256]{2,1,0:T(8,128)S(1)} custom-call(f32[6,256,128]{2,1,0:T(8,128)S(1)} %get-tuple-element.57.sums, f32[2,256,256]{2,1,0:T(8,128)S(1)} %probe_sum.2.probe), custom_call_target="tpu_custom_call" | custom-call | flops 786432 | bytes 4194304 | tf_op jit(solution)/shard_map/probe_sum/pallas_call | solution.py:326
  203.0 1.5 slice.227
  204.5 1.4 fusion.2
  (51 shorter events, 7.8 us)
Async XLA Ops:
  2.1 15.8 %copy-start.13 = (s32[2,1,1]{0,2,1:T(1,128)S(1)}, s32[2,1,1]{0,2,1:T(1,128)}, u32[]{:S(2)}) copy-start(s32[2,1,1]{0,2,1:T(1,128)} %param.19) | copy-start | bytes 28
  2.1 16.4 %copy-start.12 = (s32[2,2,12]{2,1,0:T(2,128)S(1)}, s32[2,2,12]{2,1,0:T(2,128)}, u32[]{:S(2)}) copy-start(s32[2,2,12]{2,1,0:T(2,128)} %param.18) | copy-start | bytes 580
  2.2 16.3 %copy-start.11 = (bf16[2,12,256,256]{3,2,1,0:T(8,128)(2,1)S(1)}, bf16[2,12,256,256]{3,2,1,0:T(8,128)(2,1)}, u32[]{:S(2)}) copy-start(bf16[2,12,256,256]{3,2,1,0:T(8,128)(2,1)} %param.17) | copy-start | bytes 9437188
  2.2 12.1 %collective-permute-start = (bf16[2,256,384]{2,1,0:T(8,128)(2,1)S(1)}, bf16[2,256,384]{2,1,0:T(8,128)(2,1)S(1)}, u32[]{:S(2)}, u32[]{:S(2)}) collective-permute-start(bf16[2,256,384]{2,1,0:T(8,128)(2,1)S(1)} %slice.212), channel_id=1, source_target_pairs={{4,0},{8,4},{12,8},{16,12},{20,16},{24,20},{28,24},{5,1},{9,5},{13... | collective-permute-start | bytes 1179656 | tf_op jit(solution)/shard_map/ppermute | solution.py:26
  14.4 14.2 %collective-permute-start.1 = (bf16[2,768,256]{2,1,0:T(8,128)(2,1)S(1)}, bf16[2,768,256]{2,1,0:T(8,128)(2,1)S(1)}, u32[]{:S(2)}, u32[]{:S(2)}) collective-permute-start(bf16[2,768,256]{2,1,0:T(8,128)(2,1)S(1)} %pad_maximum_fusion), channel_id=1, source_target_pairs={{1,0},{2,1},{3,2},{5,4},{6,5},{7,6},{9,8},{10,9},{11,10},{13,12},{... | collective-permute-start | bytes 2359304 | tf_op jit(solution)/shard_map/ppermute | solution.py:26
  18.8 10.0 %copy-start.7 = (f32[2,512,384]{2,1,0:T(8,128)S(1)}, f32[2,512,384]{2,1,0:T(8,128)}, u32[]{:S(2)}) copy-start(f32[2,512,384]{2,1,0:T(8,128)} %param.15) | copy-start | bytes 4718596
  28.8 2.2 %copy-start = (f32[2,256,256]{2,1,0:T(8,128)S(1)}, f32[2,256,256]{2,1,0:T(8,128)}, u32[]{:S(2)}) copy-start(f32[2,256,256]{2,1,0:T(8,128)} %probe.3) | copy-start | bytes 1572868
  28.8 2.2 %copy-start.1 = (bf16[512,512]{1,0:T(8,128)(2,1)S(1)}, bf16[512,512]{1,0:T(8,128)(2,1)}, u32[]{:S(2)}) copy-start(bf16[512,512]{1,0:T(8,128)(2,1)} %constant.102.clone.left_table) | copy-start | bytes 1572868
  28.8 2.1 %copy-start.3 = (bf16[512,512]{1,0:T(8,128)(2,1)S(1)}, bf16[512,512]{1,0:T(8,128)(2,1)}, u32[]{:S(2)}) copy-start(bf16[512,512]{1,0:T(8,128)(2,1)} %constant.103.clone.right_table) | copy-start | bytes 1572868
  43.8 10.8 %collective-permute-start.2 = (bf16[2,768,256]{2,1,0:T(8,128)(2,1)S(1)}, bf16[2,768,256]{2,1,0:T(8,128)(2,1)S(1)}, u32[]{:S(2)}, u32[]{:S(2)}) collective-permute-start(bf16[2,768,256]{2,1,0:T(8,128)(2,1)S(1)} %slice.255), channel_id=1, source_target_pairs={{0,1},{1,2},{2,3},{4,5},{5,6},{6,7},{8,9},{9,10},{10,11},{12,13},{... | collective-permute-start | bytes 2359304 | tf_op jit(solution)/shard_map/ppermute | solution.py:26
  56.2 1.4 copy-start.9
  57.7 9.5 %collective-permute-start.3 = (bf16[2,256,384]{2,1,0:T(8,128)(2,1)S(1)}, bf16[2,256,384]{2,1,0:T(8,128)(2,1)}, u32[]{:S(2)}, u32[]{:S(2)}) collective-permute-start(bf16[2,256,384]{2,1,0:T(8,128)(2,1)S(1)} %slice.257), channel_id=1, source_target_pairs={{0,4},{4,8},{8,12},{12,16},{16,20},{20,24},{24,28},{1,5},{5,9},{9,... | collective-permute-start | bytes 1179656 | tf_op jit(solution)/shard_map/ppermute | solution.py:26
  62.5 6.0 %copy-start.8 = (f32[2,512,384]{2,1,0:T(8,128)S(1)}, f32[2,512,384]{2,1,0:T(8,128)}, u32[]{:S(2)}) copy-start(f32[2,512,384]{2,1,0:T(8,128)} %param.15) | copy-start | bytes 4718596
  68.8 60.6 %copy-start.5 = (f32[2,512,384]{2,1,0:T(8,128)}, f32[2,512,384]{2,1,0:T(8,128)S(1)}, u32[]{:S(2)}) copy-start(f32[2,512,384]{2,1,0:T(8,128)S(1)} %get-tuple-element.59) | copy-start | bytes 4718596
  68.8 8.5 %collective-permute-start.4 = (bf16[2,256,384]{2,1,0:T(8,128)(2,1)S(1)}, bf16[2,256,384]{2,1,0:T(8,128)(2,1)S(1)}, u32[]{:S(2)}, u32[]{:S(2)}) collective-permute-start(bf16[2,256,384]{2,1,0:T(8,128)(2,1)S(1)} %slice.221), channel_id=1, source_target_pairs={{4,0},{8,4},{12,8},{16,12},{20,16},{24,20},{28,24},{5,1},{9,5},{13... | collective-permute-start | bytes 1179656 | tf_op jit(solution)/shard_map/ppermute | solution.py:26
  77.4 51.8 %collective-permute-start.5 = (bf16[2,768,256]{2,1,0:T(8,128)(2,1)S(1)}, bf16[2,768,256]{2,1,0:T(8,128)(2,1)S(1)}, u32[]{:S(2)}, u32[]{:S(2)}) collective-permute-start(bf16[2,768,256]{2,1,0:T(8,128)(2,1)S(1)} %pad_maximum_fusion.1), channel_id=1, source_target_pairs={{1,0},{2,1},{3,2},{5,4},{6,5},{7,6},{9,8},{10,9},{11,10},{13,12},{... | collective-permute-start | bytes 2359304 | tf_op jit(solution)/shard_map/ppermute | solution.py:26
  129.4 2.1 %copy-start.2 = (bf16[512,512]{1,0:T(8,128)(2,1)S(1)}, bf16[512,512]{1,0:T(8,128)(2,1)}, u32[]{:S(2)}) copy-start(bf16[512,512]{1,0:T(8,128)(2,1)} %constant.102.clone.left_table) | copy-start | bytes 1572868
  129.4 2.1 %copy-start.4 = (bf16[512,512]{1,0:T(8,128)(2,1)S(1)}, bf16[512,512]{1,0:T(8,128)(2,1)}, u32[]{:S(2)}) copy-start(bf16[512,512]{1,0:T(8,128)(2,1)} %constant.103.clone.right_table) | copy-start | bytes 1572868
  157.2 10.8 %collective-permute-start.6 = (bf16[2,768,256]{2,1,0:T(8,128)(2,1)S(1)}, bf16[2,768,256]{2,1,0:T(8,128)(2,1)S(1)}, u32[]{:S(2)}, u32[]{:S(2)}) collective-permute-start(bf16[2,768,256]{2,1,0:T(8,128)(2,1)S(1)} %slice.254), channel_id=1, source_target_pairs={{0,1},{1,2},{2,3},{4,5},{5,6},{6,7},{8,9},{9,10},{10,11},{12,13},{... | collective-permute-start | bytes 2359304 | tf_op jit(solution)/shard_map/ppermute | solution.py:26
  169.6 1.4 copy-start.10
  171.8 32.7 %collective-permute-start.7 = (bf16[2,256,384]{2,1,0:T(8,128)(2,1)}, bf16[2,256,384]{2,1,0:T(8,128)(2,1)}, u32[]{:S(2)}, u32[]{:S(2)}) collective-permute-start(bf16[2,256,384]{2,1,0:T(8,128)(2,1)} %slice.256), channel_id=1, source_target_pairs={{0,4},{4,8},{8,12},{12,16},{16,20},{20,24},{24,28},{1,5},{5,9},{9,... | collective-permute-start | bytes 1179656 | tf_op jit(solution)/shard_map/ppermute | solution.py:26
  204.5 1.8 copy-start.6
where the time goes:
time: 210 us; the launch traced here: 208 us
  Pallas kernels  113 us (54%)
  waiting for transfers between devices  44.1 us (21%)
  starting transfers between devices  18.2 us (9%)
  local copies, waits for them, and re-layouts  15.6 us (7%)
  other arithmetic  15 us (7%)
  between operations  2.44 us (1%)
    pallas_call x2, Pallas kernels, next_probe(): pl.pallas_call(functools.partial(probe_kernel, n_row, n_col), out_shape=j...  77.6 us
    ppermute x8, waiting for transfers between devices, passed_along(): lax.ppermute(value, axis, [(source, source + steps) for source in range(f...  44.1 us
    pallas_call x2, Pallas kernels, frame_sums(): pl.pallas_call(frames_kernel, out_shape=(jax.ShapeDtypeStruct(extended.sh...  35.5 us
    ppermute x8, starting transfers between devices, passed_along(): lax.ppermute(value, axis, [(source, source + steps) for source in range(f...  18.2 us
    reshape x2, other arithmetic, frame_sums(): extended = extended.reshape(planes, tall // SUBLANES, SUBLANES, width)  4.24 us
  transfers between devices with their start and end apart: 8, of which 6 were waited for; matrix products, arithmetic and copies ran while one was open for 4% of the time, Pallas kernels for 37%

commit v1 on v0

--- a/solution.py
+++ b/solution.py
@@ -20,12 +20,6 @@
 MESH = pl.DeviceIdType.MESH
 
 
-def passed_along(value, axis, steps):
-    count = lax.axis_size(axis)
-    first, last = (max(0, -steps), min(count, count - steps))
-    return lax.ppermute(value, axis, [(source, source + steps) for source in range(first, last)])
-
-
 def chirp_blocks(frame_size):
     offset = np.arange(frame_size, dtype=np.int32)
     differ = offset[:, None] - offset[None, :]
@@ -37,10 +31,43 @@
 
 
 def frames_kernel(
-    positions, live, extended, probe, amplitudes, left_table, right_table, gathered, sums
+    positions,
+    live,
+    block,
+    below,
+    beside,
+    corner,
+    probe,
+    amplitudes,
+    left_table,
+    right_table,
+    own_grad,
+    below_grad,
+    beside_grad,
+    corner_grad,
+    sums,
+    extended,
+    gathered,
 ):
     size = probe.shape[-1]
     halves = size // LANES
+    block_rows, block_columns = block.shape[1:]
+    regions = (
+        (block, own_grad, slice(0, block_rows), slice(0, block_columns)),
+        (below, below_grad, slice(block_rows, None), slice(0, block_columns)),
+        (beside, beside_grad, slice(0, block_rows), slice(block_columns, None)),
+        (corner, corner_grad, slice(block_rows, None), slice(block_columns, None)),
+    )
+
+    def grouped(rows):
+        stop = None if rows.stop is None else rows.stop // SUBLANES
+        return slice(rows.start // SUBLANES, stop)
+
+    for source, _, rows, lanes in regions:
+        planes, tall, width = source.shape
+        extended[:, grouped(rows), :, lanes] = (
+            source[...].astype(jnp.float32).reshape(planes, tall // SUBLANES, SUBLANES, width)
+        )
     gathered[...] = jnp.zeros_like(gathered)
     sums[...] = jnp.zeros_like(sums)
     groups = size // SUBLANES
@@ -53,14 +80,14 @@
     def one_frame(slot, weight):
         top = positions[0, slot]
         left = positions[1, slot]
-        block = left // LANES
-        shift = left - block * LANES
+        column_block = left // LANES
+        shift = left - column_block * LANES
         row_block = top // SUBLANES
         row_shift = top - row_block * SUBLANES
         rows = pl.ds(row_block, groups + 1)
 
         def columns(part):
-            return pl.ds(pl.multiple_of((block + part) * LANES, LANES), LANES)
+            return pl.ds(pl.multiple_of((column_block + part) * LANES, LANES), LANES)
 
         patch = []
         back_shift = lax.rem(LANES - shift, LANES)
@@ -153,23 +180,29 @@
         return carry
 
     lax.fori_loop(0, (count + 1) // 2, pair, 0)
-
-
-def frame_sums(extended, probe_field, amplitudes, positions, live, tables):
+    for _, target, rows, lanes in regions:
+        target[...] = (
+            gathered[:, grouped(rows), :, lanes].reshape(target.shape).astype(target.dtype)
+        )
+
+
+def frame_sums(block, rims, probe_field, amplitudes, positions, live, tables):
     size = probe_field.shape[-1]
     slots = amplitudes.shape[0]
     vmem = pl.BlockSpec(memory_space=pltpu.VMEM)
     smem = pl.BlockSpec(memory_space=pltpu.SMEM)
-    planes, tall, width = extended.shape
-    extended = extended.reshape(planes, tall // SUBLANES, SUBLANES, width)
-    gathered, sums = pl.pallas_call(
+    planes, rows, columns = block.shape
+    whole = (planes, (rows + size) // SUBLANES, SUBLANES, columns + size)
+    return pl.pallas_call(
         frames_kernel,
         out_shape=(
-            jax.ShapeDtypeStruct(extended.shape, jnp.float32),
+            jax.ShapeDtypeStruct(block.shape, jnp.float32),
+            *[jax.ShapeDtypeStruct(rim.shape, jnp.bfloat16) for rim in rims],
             jax.ShapeDtypeStruct((3 * size // LANES, size, LANES), jnp.float32),
         ),
-        in_specs=[smem, smem] + [vmem] * 5,
-        out_specs=(vmem, vmem),
+        in_specs=[smem, smem] + [vmem] * 8,
+        out_specs=(vmem,) * 5,
+        scratch_shapes=[pltpu.VMEM(whole, jnp.float32), pltpu.VMEM(whole, jnp.float32)],
         compiler_params=pltpu.CompilerParams(vmem_limit_bytes=48 * 1024 * 1024),
         cost_estimate=pl.CostEstimate(
             flops=slots * 32 * size**3,
@@ -177,38 +210,154 @@
             transcendentals=slots * size * size,
         ),
         name="frames",
-    )(positions, live, extended, probe_field, amplitudes, *tables)
-    return gathered.reshape(planes, tall, width), sums
-
-
-def probe_kernel(
-    n_row,
-    n_col,
-    sums,
-    probe,
-    out,
-    wide,
-    got_col,
-    own_rows,
-    got_row,
-    piece,
-    steps,
-    joined,
-    got_steps,
-    col_send,
-    col_recv,
-    row_send,
-    row_recv,
-    back_row_send,
-    back_row_recv,
-    back_col_send,
-    back_col_recv,
-):
-    row, col = lax.axis_index("row"), lax.axis_index("col")
+    )(positions, live, block, *rims, probe_field, amplitudes, *tables)
+
+
+def remote(source, target, send, recv, device):
+    return pltpu.make_async_remote_copy(
+        src_ref=source,
+        dst_ref=target,
+        send_sem=send,
+        recv_sem=recv,
+        device_id=device,
+        device_id_type=MESH,
+    )
+
+
+class Neighbours:
+
+    def __init__(self, n_row, n_col):
+        self.row, self.col = lax.axis_index("row"), lax.axis_index("col")
+        self.above, self.under = self.row > 0, self.row < n_row - 1
+        self.left, self.right = self.col > 0, self.col < n_col - 1
+
+    def back(self):
+        row, col = self.row, self.col
+        return (
+            (self.above, (row - 1, col)),
+            (self.left, (row, col - 1)),
+            (jnp.logical_and(self.above, self.left), (row - 1, col - 1)),
+        )
+
+    def ahead(self):
+        row, col = self.row, self.col
+        return (
+            (self.under, (row + 1, col)),
+            (self.right, (row, col + 1)),
+            (jnp.logical_and(self.under, self.right), (row + 1, col + 1)),
+        )
+
+
+def greet(barrier, device):
+    pl.semaphore_signal(barrier, inc=1, device_id=device, device_id_type=MESH)
+
+
+def how_many(neighbours):
+    return sum(there.astype(jnp.int32) for there, _ in neighbours)
+
+
+def send_halos(near, narrow, rims, send, recv):
+    _, height, _ = rims[0].shape
+    _, _, width = rims[1].shape
+    sources = (
+        narrow.at[:, :height, :],
+        narrow.at[:, :, :width],
+        narrow.at[:, :height, :width],
+    )
+    sent = []
+    for index, (there, device) in enumerate(near.back()):
+        copy = remote(sources[index], rims[index], send.at[index], recv.at[index], device)
+        pl.when(there)(copy.start)
+        sent.append(copy)
+
+    def finish():
+        for copy, (there, _) in zip(sent, near.ahead()):
+            pl.when(there)(copy.wait_recv)
+        for copy, (there, _) in zip(sent, near.back()):
+            pl.when(there)(copy.wait_send)
+
+    return finish
+
+
+def halo_kernel(n_row, n_col, block, below, beside, corner, narrow, send, recv):
+    near = Neighbours(n_row, n_col)
+    barrier = pltpu.get_barrier_semaphore()
+    for there, device in near.back() + near.ahead():
+        pl.when(there)(functools.partial(greet, barrier, device))
+    narrow[...] = block[...].astype(jnp.bfloat16)
+    pl.semaphore_wait(barrier, how_many(near.back() + near.ahead()))
+    send_halos(near, narrow, (below, beside, corner), send, recv)()
+
+
+def rim_shapes(block, size):
+    planes, rows, columns = block.shape
+    return tuple(
+        jax.ShapeDtypeStruct(shape, jnp.bfloat16)
+        for shape in ((planes, size, columns), (planes, rows, size), (planes, size, size))
+    )
+
+
+def first_halos(block, size):
+    n_row, n_col = lax.axis_size("row"), lax.axis_size("col")
+    hbm = pl.BlockSpec(memory_space=pl.ANY)
+    dma = pltpu.SemaphoreType.DMA
+    return pl.pallas_call(
+        functools.partial(halo_kernel, n_row, n_col),
+        out_shape=rim_shapes(block, size),
+        in_specs=[pl.BlockSpec(memory_space=pltpu.VMEM)],
+        out_specs=(hbm,) * 3,
+        scratch_shapes=[pltpu.VMEM(block.shape, jnp.bfloat16), dma((3,)), dma((3,))],
+        compiler_params=pltpu.CompilerParams(
+            collective_id=0, has_side_effects=True, vmem_limit_bytes=32 * 1024 * 1024
+        ),
+        cost_estimate=pl.CostEstimate(
+            flops=block.size, bytes_accessed=4 * 1024 * 1024, transcendentals=0
+        ),
+        name="first_halos",
+    )(block)
+
+
+def exchange_kernel(n_row, n_col, halos, *refs):
+    block, own_grad, below_grad, beside_grad, corner_grad, sums, probe = refs[:7]
+    refs = refs[7:]
+    rims = ()
+    new_block, out = refs[:2]
+    refs = refs[2:]
+    if halos:
+        rims, refs = refs[:3], refs[3:]
+    (
+        got_below,
+        got_beside,
+        got_corner,
+        narrow,
+        wide,
+        got_col,
+        own_rows,
+        got_row,
+        piece,
+        steps,
+        joined,
+        got_steps,
+        grad_send,
+        grad_recv,
+        halo_send,
+        halo_recv,
+        col_send,
+        col_recv,
+        row_send,
+        row_recv,
+        back_row_send,
+        back_row_recv,
+        back_col_send,
+        back_col_recv,
+    ) = refs
+    near = Neighbours(n_row, n_col)
+    row, col = near.row, near.col
     planes, size, _ = sums.shape
     chunk = size // n_col
     part = chunk // n_row
-    comps = planes * 2 // 3
+    halves = planes // 3
+    comps = 2 * halves
 
     def along_col(step):
         return (row, lax.rem(col + step, n_col))
@@ -218,21 +367,17 @@
 
     barrier = pltpu.get_barrier_semaphore()
     for step in range(1, n_col):
-        pl.semaphore_signal(barrier, inc=1, device_id=along_col(step), device_id_type=MESH)
+        greet(barrier, along_col(step))
     for step in range(1, n_row):
-        pl.semaphore_signal(barrier, inc=1, device_id=along_row(step), device_id_type=MESH)
+        greet(barrier, along_row(step))
+    corners = (near.back()[2], near.ahead()[2])
+    for there, device in corners:
+        pl.when(there)(functools.partial(greet, barrier, device))
     wide[...] = sums[...].astype(jnp.bfloat16)
-    pl.semaphore_wait(barrier, n_col + n_row - 2)
-
-    def remote(source, target, send, recv, device):
-        copy = pltpu.make_async_remote_copy(
-            src_ref=source,
-            dst_ref=target,
-            send_sem=send,
-            recv_sem=recv,
-            device_id=device,
-            device_id_type=MESH,
-        )
+    pl.semaphore_wait(barrier, n_col + n_row - 2 + how_many(corners))
+
+    def started(source, target, send, recv, device):
+        copy = remote(source, target, send, recv, device)
         copy.start()
         return copy
 
@@ -243,7 +388,7 @@
     for step in range(1, n_col):
         their = lax.rem(col + step, n_col)
         first.append(
-            remote(
+            started(
                 wide.at[:, rows_of(their, chunk), :],
                 got_col.at[step - 1],
                 col_send.at[step - 1],
@@ -251,6 +396,16 @@
                 along_col(step),
             )
         )
+    grads = []
+    pairs = ((below_grad, got_below), (beside_grad, got_beside), (corner_grad, got_corner))
+    for index, (there, device) in enumerate(near.ahead()):
+        source, target = pairs[index]
+        copy = remote(source, target, grad_send.at[index], grad_recv.at[index], device)
+        pl.when(there)(copy.start)
+        grads.append(copy)
+    step_size = ALPHA / (jnp.max(probe[0] * probe[0] + probe[1] * probe[1]) + 1e-06)
+    new_block[...] = block[...] - step_size * own_grad[...]
+
     total = sums[:, rows_of(col, chunk), :]
     for step, copy in enumerate(first):
         copy.wait_recv()
@@ -261,7 +416,7 @@
     for step in range(1, n_row):
         their = lax.rem(row + step, n_row)
         second.append(
-            remote(
+            started(
                 own_rows.at[their],
                 got_row.at[step - 1],
                 row_send.at[step - 1],
@@ -269,17 +424,31 @@
                 along_row(step),
             )
         )
+
+    for index, (there, _) in enumerate(near.back()):
+        target = pairs[index][1]
+        copy = grads[index]
+        _, height, width = target.shape
+
+        def add_rim():
+            copy.wait_recv()
+            new_block[:, :height, :width] -= step_size * target[...].astype(jnp.float32)
+
+        pl.when(there)(add_rim)
+    if halos:
+        narrow[...] = new_block[...].astype(jnp.bfloat16)
+        finish_halos = send_halos(near, narrow, rims, halo_send, halo_recv)
+
     total = own_rows[row]
     for step, copy in enumerate(second):
         copy.wait_recv()
         total = total + got_row[step]
-    halves = planes // 3
     weight = total[2 * halves :] + 1.0
     piece[...] = jnp.concatenate(
         [total[:halves] / weight, total[halves : 2 * halves] / weight], axis=0
     )
     third = [
-        remote(
+        started(
             piece,
             steps.at[row],
             back_row_send.at[step - 1],
@@ -293,7 +462,7 @@
         copy.wait_recv()
     joined[...] = jnp.concatenate([steps[index] for index in range(n_row)], axis=1)
     fourth = [
-        remote(
+        started(
             joined,
             got_steps.at[col],
             back_col_send.at[step - 1],
@@ -313,22 +482,35 @@
             out[comp, rows, lanes] = probe[comp, rows, lanes] - got_steps[index, plane]
     for copy in first + second + third + fourth:
         copy.wait_send()
-
-
-def next_probe(sums, probe_field):
+    for copy, (there, _) in zip(grads, near.ahead()):
+        pl.when(there)(copy.wait_send)
+    if halos:
+        finish_halos()
+
+
+def exchange(block, own_grad, grad_rims, sums, probe_field, halos):
     n_row, n_col = lax.axis_size("row"), lax.axis_size("col")
     planes, size, _ = sums.shape
     chunk = size // n_col
     part = chunk // n_row
     comps = planes * 2 // 3
     vmem = pl.BlockSpec(memory_space=pltpu.VMEM)
+    hbm = pl.BlockSpec(memory_space=pl.ANY)
     dma = pltpu.SemaphoreType.DMA
-    return pl.pallas_call(
-        functools.partial(probe_kernel, n_row, n_col),
-        out_shape=jax.ShapeDtypeStruct(probe_field.shape, jnp.float32),
-        in_specs=[vmem, vmem],
-        out_specs=vmem,
+    shapes = rim_shapes(block, size)
+    fresh = shapes if halos else ()
+    new_block, new_probe, *rims = pl.pallas_call(
+        functools.partial(exchange_kernel, n_row, n_col, halos),
+        out_shape=(
+            jax.ShapeDtypeStruct(block.shape, jnp.float32),
+            jax.ShapeDtypeStruct(probe_field.shape, jnp.float32),
+            *fresh,
+        ),
+        in_specs=[vmem, vmem, hbm, hbm, hbm, vmem, vmem],
+        out_specs=(vmem, vmem) + (hbm,) * len(fresh),
         scratch_shapes=[
+            *[pltpu.VMEM(shape.shape, shape.dtype) for shape in shapes],
+            pltpu.VMEM(block.shape, jnp.bfloat16),
             pltpu.VMEM(sums.shape, jnp.bfloat16),
             pltpu.VMEM((n_col - 1, planes, chunk, LANES), jnp.bfloat16),
             pltpu.VMEM((n_row, planes, part, LANES), jnp.float32),
@@ -337,6 +519,10 @@
             pltpu.VMEM((n_row, comps, part, LANES), jnp.float32),
             pltpu.VMEM((comps, chunk, LANES), jnp.float32),
             pltpu.VMEM((n_col, comps, chunk, LANES), jnp.float32),
+            dma((3,)),
+            dma((3,)),
+            dma((3,)),
+            dma((3,)),
             dma((n_col - 1,)),
             dma((n_col - 1,)),
             dma((n_row - 1,)),
@@ -347,55 +533,35 @@
             dma((n_col - 1,)),
         ],
         compiler_params=pltpu.CompilerParams(
-            collective_id=0, has_side_effects=True, vmem_limit_bytes=32 * 1024 * 1024
+            collective_id=1 if halos else 2,
+            has_side_effects=True,
+            vmem_limit_bytes=48 * 1024 * 1024,
         ),
         cost_estimate=pl.CostEstimate(
-            flops=planes * size * LANES * 4, bytes_accessed=4 * 1024 * 1024, transcendentals=0
-        ),
-        name="probe_sum",
-    )(sums, probe_field)
-
-
-def extend_block(object_field, frame_size):
-    below = passed_along(object_field[:, :frame_size, :].astype(jnp.bfloat16), "row", -1)
-    taller = jnp.concatenate([object_field[:, :, :frame_size].astype(jnp.bfloat16), below[:, :, :frame_size]], axis=1)
-    beside = passed_along(taller, "col", -1).astype(jnp.float32)
-    own = jnp.concatenate([object_field, below.astype(jnp.float32)], axis=1)
-    return jnp.concatenate([own, beside], axis=2)
-
-
-def fold_rims(gathered, block_rows, block_columns):
-    from_left = passed_along(gathered[:, :, block_columns:].astype(jnp.bfloat16), "col", 1).astype(
-        jnp.float32
-    )
-    narrow = gathered[:, :, :block_columns]
-    narrow = narrow.at[:, :, : from_left.shape[2]].add(from_left)
-    from_above = passed_along(narrow[:, block_rows:, :].astype(jnp.bfloat16), "row", 1).astype(
-        jnp.float32
-    )
-    return narrow[:, :block_rows, :].at[:, : from_above.shape[1], :].add(from_above)
+            flops=planes * size * LANES * 4, bytes_accessed=8 * 1024 * 1024, transcendentals=0
+        ),
+        name="exchange",
+    )(block, own_grad, *grad_rims, sums, probe_field)
+    return new_block, new_probe, tuple(rims)
 
 
 def local(object_field, probe_field, amplitudes, positions, live_counts):
     frame_size = probe_field.shape[-1]
-    block_rows, block_columns = (object_field.shape[1], object_field.shape[2])
     tables = chirp_blocks(frame_size)
+    rims = first_halos(object_field, frame_size)
     for iteration in range(ITERS):
-        extended = extend_block(object_field, frame_size)
-        gathered, sums = frame_sums(
-            extended,
+        own_grad, *grad_rims, sums = frame_sums(
+            object_field,
+            rims,
             probe_field,
             amplitudes[iteration],
             positions[iteration],
             live_counts[iteration, 0],
             tables,
         )
-        object_sum = fold_rims(gathered, block_rows, block_columns)
-        step_size = ALPHA / (
-            jnp.max(probe_field[0] * probe_field[0] + probe_field[1] * probe_field[1]) + 1e-06
-        )
-        object_field = object_field - step_size * object_sum
-        probe_field = next_probe(sums, probe_field)
+        object_field, probe_field, rims = exchange(
+            object_field, own_grad, grad_rims, sums, probe_field, iteration < ITERS - 1
+        )
     return (object_field, probe_field)
 
 

time: 210 us -> 156 us (0.74)
  the two profiles are of different devices: /device:TPU:25 before, /device:TPU:0 now
where the time goes in v1:
time: 156 us
  Pallas kernels  145 us (93%)
  local copies, waits for them, and re-layouts  10.5 us (7%)
    pallas_call x2, Pallas kernels, exchange(): pl.pallas_call(functools.partial(exchange_kernel, n_row, n_col, halos), o...  97.1 us
    pallas_call x2, Pallas kernels, frame_sums(): pl.pallas_call(frames_kernel, out_shape=(jax.ShapeDtypeStruct(block.shape...  30.3 us
    pallas_call x1, Pallas kernels, first_halos(): pl.pallas_call(functools.partial(halo_kernel, n_row, n_col), out_shape=ri...  17.3 us
    unnamed x14, local copies, waits for them, and re-layouts  4.52 us
    squeeze x1, local copies, waits for them, and re-layouts, local(): amplitudes[iteration]  3.98 us

profile of v1, /device:TPU:0, one launch (start us, length us, event | category | flops | bytes accessed | tf_op | source)
XLA Modules:
  0.0 155.9 jit_solution(5947431590989115733)
XLA Ops:
  0.6 1.3 fusion
  1.9 0.7 slice_bitcast_fusion.2
  2.6 0.0 copy-start
  2.6 1.4 copy-done
  4.0 17.3 %first_halos.1 = (bf16[2,256,384]{2,1,0:T(8,128)(2,1)S(1)}, bf16[2,512,256]{2,1,0:T(8,128)(2,1)S(1)}, bf16[2,256,256]{2,1,0:T(8,128)(2,1)S(1)}) custom-call(f32[2,512,384]{2,1,0:T(8,128)S(1)} %copy-done), custom_call_target="tpu_custom_call" | custom-call | flops 393216 | bytes 4194304 | tf_op jit(solution)/shard_map/first_halos/pallas_call | solution.py:304
  21.4 0.0 copy-start.3
  21.4 0.0 copy-start.4
  21.4 0.0 copy-start.5
  21.4 4.0 %slice_bitcast_fusion = (bf16[12,256,256]{2,1,0:T(8,128)(2,1)}, bf16[12,256,256]{2,1,0:T(8,128)(2,1)}) fusion(bf16[2,12,256,256]{3,2,1,0:T(8,128)(2,1)} %param.9), kind=kLoop, calls=%fused_computation | loop fusion | bytes 6291456 | tf_op jit(solution)/shard_map/squeeze | solution.py:557
  25.4 0.0 copy-done.3
  25.4 0.0 copy-done.4
  25.4 0.0 copy-done.5
  25.4 22.7 %frames.2 = (f32[2,512,384]{2,1,0:T(8,128)}, bf16[2,256,384]{2,1,0:T(8,128)(2,1)S(1)}, bf16[2,512,256]{2,1,0:T(8,128)(2,1)S(1)}, bf16[2,256,256]{2,1,0:T(8,128)(2,1)S(1)}, f32[6,256,128]{2,1,0:T(8,128)S(1)}) custom-call(s32[2,12]{1,0:T(2,128)S(1)} %get-tuple-element.41.positions, s32[1]{0:T(128)} %bitcast.1.live, f32[2,512,384]{2,1,0:T(8,128)} %refs_0_.1, ...), custom_call_target="tpu_custom_call" | custom-call | flops 6442450944 | bytes 12582912 | tf_op jit(solution)/shard_map/frames/pallas_call | solution.py:196
  48.1 47.6 %exchange.2 = (f32[2,512,384]{2,1,0:T(8,128)S(1)}, f32[2,256,256]{2,1,0:T(8,128)S(1)}, bf16[2,256,384]{2,1,0:T(8,128)(2,1)S(1)}, bf16[2,512,256]{2,1,0:T(8,128)(2,1)S(1)}, bf16[2,256,256]{2,1,0:T(8,128)(2,1)S(1)}) custom-call(f32[2,512,384]{2,1,0:T(8,128)} %refs_0_.1, f32[2,512,384]{2,1,0:T(8,128)} %get-tuple-element.23.refs_1_, ...), custom_call_target="tpu_custom_call" | custom-call | flops 786432 | bytes 8388608 | tf_op jit(solution)/shard_map/exchange/pallas_call | solution.py:502
  95.7 0.0 copy-start.1
  95.7 1.2 copy-done.1
  96.9 0.0 copy-start.2
  96.9 7.5 %frames.3 = (f32[2,512,384]{2,1,0:T(8,128)}, bf16[2,256,384]{2,1,0:T(8,128)(2,1)S(1)}, bf16[2,512,256]{2,1,0:T(8,128)(2,1)S(1)}, bf16[2,256,256]{2,1,0:T(8,128)(2,1)S(1)}, f32[6,256,128]{2,1,0:T(8,128)S(1)}) custom-call(s32[2,12]{1,0:T(2,128)S(1)} %get-tuple-element.40.positions, s32[1]{0:T(128)} %bitcast.4.live, f32[2,512,384]{2,1,0:T(8,128)} %copy-done.1, ...), custom_call_target="tpu_custom_call" | custom-call | flops 6442450944 | bytes 12582912 | tf_op jit(solution)/shard_map/frames/pallas_call | solution.py:196
  104.4 0.0 copy-done.2
  104.4 49.5 %exchange.3 = (f32[2,512,384]{2,1,0:T(8,128)S(1)}, f32[2,256,256]{2,1,0:T(8,128)S(1)}) custom-call(f32[2,512,384]{2,1,0:T(8,128)S(1)} %copy-done.2, f32[2,512,384]{2,1,0:T(8,128)} %get-tuple-element.33.refs_1_, bf16[2,256,384]{2,1,0:T(8,128)(2,1)S(1)} %get-tuple-element.34.refs_2_, bf16[2,512,256]{2,1,0:T(8,128)(2,1)S(1)} %get-tuple-element.35.refs_3_, ...), custom_call_target="tpu_custom_call" | custom-call | flops 786432 | bytes 8388608 | tf_op jit(solution)/shard_map/exchange/pallas_call | solution.py:502
  154.0 1.1 copy.11
  155.1 0.8 copy.12
Async XLA Ops:
  2.6 1.4 copy-start
  21.4 4.0 %copy-start.3 = (f32[2,256,256]{2,1,0:T(8,128)S(1)}, f32[2,256,256]{2,1,0:T(8,128)}, u32[]{:S(2)}) copy-start(f32[2,256,256]{2,1,0:T(8,128)} %refs_6_.1) | copy-start | bytes 1572868
  21.4 4.0 %copy-start.4 = (bf16[512,512]{1,0:T(8,128)(2,1)S(1)}, bf16[512,512]{1,0:T(8,128)(2,1)}, u32[]{:S(2)}) copy-start(bf16[512,512]{1,0:T(8,128)(2,1)} %constant.5.clone.right_table) | copy-start | bytes 1572868
  21.4 4.0 %copy-start.5 = (bf16[512,512]{1,0:T(8,128)(2,1)S(1)}, bf16[512,512]{1,0:T(8,128)(2,1)}, u32[]{:S(2)}) copy-start(bf16[512,512]{1,0:T(8,128)(2,1)} %constant.4.clone.left_table) | copy-start | bytes 1572868
  95.7 1.2 copy-start.1
  96.9 7.5 %copy-start.2 = (f32[2,512,384]{2,1,0:T(8,128)S(1)}, f32[2,512,384]{2,1,0:T(8,128)}, u32[]{:S(2)}) copy-start(f32[2,512,384]{2,1,0:T(8,128)} %copy-done.1) | copy-start | bytes 4718596

commit v2 on v1

--- a/solution.py
+++ b/solution.py
@@ -30,17 +30,24 @@
     return jnp.asarray(forward), jnp.asarray(forward.T.copy())
 
 
+def local_copy(source, target, semaphore):
+    copy = pltpu.make_async_copy(source, target, semaphore)
+    copy.start()
+    return copy
+
+
 def frames_kernel(
+    iteration,
     positions,
     live,
     block,
     below,
     beside,
     corner,
-    probe,
-    amplitudes,
-    left_table,
-    right_table,
+    probe_hbm,
+    amplitudes_hbm,
+    left_hbm,
+    right_hbm,
     own_grad,
     below_grad,
     beside_grad,
@@ -48,28 +55,48 @@
     sums,
     extended,
     gathered,
+    below_held,
+    beside_held,
+    corner_held,
+    probe,
+    amplitudes,
+    left_table,
+    right_table,
+    semaphores,
 ):
     size = probe.shape[-1]
     halves = size // LANES
-    block_rows, block_columns = block.shape[1:]
+    _, row_groups, _, block_columns = block.shape
+    inner = (slice(None), slice(0, row_groups), slice(None), slice(0, block_columns))
     regions = (
-        (block, own_grad, slice(0, block_rows), slice(0, block_columns)),
-        (below, below_grad, slice(block_rows, None), slice(0, block_columns)),
-        (beside, beside_grad, slice(0, block_rows), slice(block_columns, None)),
-        (corner, corner_grad, slice(block_rows, None), slice(block_columns, None)),
-    )
-
-    def grouped(rows):
-        stop = None if rows.stop is None else rows.stop // SUBLANES
-        return slice(rows.start // SUBLANES, stop)
-
-    for source, _, rows, lanes in regions:
-        planes, tall, width = source.shape
-        extended[:, grouped(rows), :, lanes] = (
-            source[...].astype(jnp.float32).reshape(planes, tall // SUBLANES, SUBLANES, width)
-        )
+        (below_held, below_grad, slice(row_groups, None), slice(0, block_columns)),
+        (beside_held, beside_grad, slice(0, row_groups), slice(block_columns, None)),
+        (corner_held, corner_grad, slice(row_groups, None), slice(block_columns, None)),
+    )
+    moves = (
+        (below, below_held),
+        (beside, beside_held),
+        (corner, corner_held),
+        (block, extended.at[inner]),
+        (probe_hbm, probe),
+        (left_hbm, left_table),
+        (amplitudes_hbm.at[iteration], amplitudes),
+        (right_hbm, right_table),
+    )
+    copies = [
+        local_copy(source, target, semaphores.at[index])
+        for index, (source, target) in enumerate(moves)
+    ]
     gathered[...] = jnp.zeros_like(gathered)
     sums[...] = jnp.zeros_like(sums)
+    for copy, (source, _, groups, lanes) in zip(copies, regions):
+        copy.wait()
+        planes, tall, width = source.shape
+        extended[:, groups, :, lanes] = (
+            source[...].astype(jnp.float32).reshape(planes, tall // SUBLANES, SUBLANES, width)
+        )
+    for copy in copies[len(regions) :]:
+        copy.wait()
     groups = size // SUBLANES
     lane = lax.broadcasted_iota(jnp.int32, (groups + 1, SUBLANES, LANES), 2)
     sublane = lax.broadcasted_iota(jnp.int32, (groups, SUBLANES, LANES), 1)
@@ -78,8 +105,8 @@
         return jnp.dot(a, b, preferred_element_type=jnp.float32)
 
     def one_frame(slot, weight):
-        top = positions[0, slot]
-        left = positions[1, slot]
+        top = positions[iteration, 0, slot]
+        left = positions[iteration, 1, slot]
         column_block = left // LANES
         shift = left - column_block * LANES
         row_block = top // SUBLANES
@@ -172,7 +199,7 @@
                     moved, after[part], before[part]
                 )
 
-    count = live[0]
+    count = live[iteration, 0, 0]
 
     def pair(index, carry):
         one_frame(2 * index, jnp.float32(1.0))
@@ -180,29 +207,36 @@
         return carry
 
     lax.fori_loop(0, (count + 1) // 2, pair, 0)
-    for _, target, rows, lanes in regions:
-        target[...] = (
-            gathered[:, grouped(rows), :, lanes].reshape(target.shape).astype(target.dtype)
-        )
-
-
-def frame_sums(block, rims, probe_field, amplitudes, positions, live, tables):
+    leaving = local_copy(gathered.at[inner], own_grad, semaphores.at[0])
+    for _, target, groups, lanes in regions:
+        target[...] = gathered[:, groups, :, lanes].reshape(target.shape).astype(target.dtype)
+    leaving.wait()
+
+
+def frame_sums(block, rims, probe_field, amplitudes, positions, live, tables, iteration):
     size = probe_field.shape[-1]
-    slots = amplitudes.shape[0]
+    slots = amplitudes.shape[1]
     vmem = pl.BlockSpec(memory_space=pltpu.VMEM)
     smem = pl.BlockSpec(memory_space=pltpu.SMEM)
-    planes, rows, columns = block.shape
-    whole = (planes, (rows + size) // SUBLANES, SUBLANES, columns + size)
+    hbm = pl.BlockSpec(memory_space=pl.ANY)
+    planes, row_groups, _, columns = block.shape
+    whole = (planes, row_groups + size // SUBLANES, SUBLANES, columns + size)
+    held = [*rims, probe_field, amplitudes[0], *tables]
     return pl.pallas_call(
-        frames_kernel,
+        functools.partial(frames_kernel, iteration),
         out_shape=(
             jax.ShapeDtypeStruct(block.shape, jnp.float32),
             *[jax.ShapeDtypeStruct(rim.shape, jnp.bfloat16) for rim in rims],
             jax.ShapeDtypeStruct((3 * size // LANES, size, LANES), jnp.float32),
         ),
-        in_specs=[smem, smem] + [vmem] * 8,
-        out_specs=(vmem,) * 5,
-        scratch_shapes=[pltpu.VMEM(whole, jnp.float32), pltpu.VMEM(whole, jnp.float32)],
+        in_specs=[smem, smem] + [hbm] * 8,
+        out_specs=(hbm,) + (vmem,) * 4,
+        scratch_shapes=[
+            pltpu.VMEM(whole, jnp.float32),
+            pltpu.VMEM(whole, jnp.float32),
+            *[pltpu.VMEM(value.shape, value.dtype) for value in held],
+            pltpu.SemaphoreType.DMA((8,)),
+        ],
         compiler_params=pltpu.CompilerParams(vmem_limit_bytes=48 * 1024 * 1024),
         cost_estimate=pl.CostEstimate(
             flops=slots * 32 * size**3,
@@ -318,7 +352,7 @@
 
 
 def exchange_kernel(n_row, n_col, halos, *refs):
-    block, own_grad, below_grad, beside_grad, corner_grad, sums, probe = refs[:7]
+    block_hbm, own_grad_hbm, below_grad, beside_grad, corner_grad, sums_hbm, probe_hbm = refs[:7]
     refs = refs[7:]
     rims = ()
     new_block, out = refs[:2]
@@ -326,6 +360,11 @@
     if halos:
         rims, refs = refs[:3], refs[3:]
     (
+        block,
+        own_grad,
+        sums,
+        probe,
+        load,
         got_below,
         got_beside,
         got_corner,
@@ -350,7 +389,15 @@
         back_row_recv,
         back_col_send,
         back_col_recv,
+        core_send,
+        core_recv,
     ) = refs
+    loads = [
+        local_copy(source, target, load.at[index])
+        for index, (source, target) in enumerate(
+            ((sums_hbm, sums), (probe_hbm, probe), (block_hbm, block), (own_grad_hbm, own_grad))
+        )
+    ]
     near = Neighbours(n_row, n_col)
     row, col = near.row, near.col
     planes, size, _ = sums.shape
@@ -373,6 +420,7 @@
     corners = (near.back()[2], near.ahead()[2])
     for there, device in corners:
         pl.when(there)(functools.partial(greet, barrier, device))
+    loads[0].wait()
     wide[...] = sums[...].astype(jnp.bfloat16)
     pl.semaphore_wait(barrier, n_col + n_row - 2 + how_many(corners))
 
@@ -403,6 +451,8 @@
         copy = remote(source, target, grad_send.at[index], grad_recv.at[index], device)
         pl.when(there)(copy.start)
         grads.append(copy)
+    for copy in loads[1:]:
+        copy.wait()
     step_size = ALPHA / (jnp.max(probe[0] * probe[0] + probe[1] * probe[1]) + 1e-06)
     new_block[...] = block[...] - step_size * own_grad[...]
 
@@ -425,20 +475,6 @@
             )
         )
 
-    for index, (there, _) in enumerate(near.back()):
-        target = pairs[index][1]
-        copy = grads[index]
-        _, height, width = target.shape
-
-        def add_rim():
-            copy.wait_recv()
-            new_block[:, :height, :width] -= step_size * target[...].astype(jnp.float32)
-
-        pl.when(there)(add_rim)
-    if halos:
-        narrow[...] = new_block[...].astype(jnp.bfloat16)
-        finish_halos = send_halos(near, narrow, rims, halo_send, halo_recv)
-
     total = own_rows[row]
     for step, copy in enumerate(second):
         copy.wait_recv()
@@ -461,18 +497,42 @@
     for copy in third:
         copy.wait_recv()
     joined[...] = jnp.concatenate([steps[index] for index in range(n_row)], axis=1)
-    fourth = [
+    got_steps[col] = joined[...]
+    count = n_col // 2
+    place, core = col // 2, lax.rem(col, 2)
+    other = (row, col + 1 - 2 * core)
+    across = [
         started(
             joined,
             got_steps.at[col],
             back_col_send.at[step - 1],
             back_col_recv.at[step - 1],
-            along_col(step),
-        )
-        for step in range(1, n_col)
+            (row, lax.rem(place + step, count) * 2 + core),
+        )
+        for step in range(1, count)
     ]
-    got_steps[col] = joined[...]
-    for copy in fourth:
+    over = [started(joined, got_steps.at[col], core_send.at[0], core_recv.at[0], other)]
+
+    for index, (there, _) in enumerate(near.back()):
+        target = pairs[index][1]
+        copy = grads[index]
+        _, height, width = target.shape
+
+        def add_rim():
+            copy.wait_recv()
+            new_block[:, :height, :width] -= step_size * target[...].astype(jnp.float32)
+
+        pl.when(there)(add_rim)
+    if halos:
+        narrow[...] = new_block[...].astype(jnp.bfloat16)
+        finish_halos = send_halos(near, narrow, rims, halo_send, halo_recv)
+
+
+    for step in range(1, count):
+        across[step - 1].wait_recv()
+        slot = got_steps.at[lax.rem(place + count - step, count) * 2 + core]
+        over.append(started(slot, slot, core_send.at[step], core_recv.at[step], other))
+    for copy in over:
         copy.wait_recv()
     for index in range(n_col):
         rows = slice(index * chunk, (index + 1) * chunk)
@@ -480,7 +540,7 @@
             comp, half = divmod(plane, halves)
             lanes = slice(half * LANES, (half + 1) * LANES)
             out[comp, rows, lanes] = probe[comp, rows, lanes] - got_steps[index, plane]
-    for copy in first + second + third + fourth:
+    for copy in first + second + third + across + over:
         copy.wait_send()
     for copy, (there, _) in zip(grads, near.ahead()):
         pl.when(there)(copy.wait_send)
@@ -506,9 +566,11 @@
             jax.ShapeDtypeStruct(probe_field.shape, jnp.float32),
             *fresh,
         ),
-        in_specs=[vmem, vmem, hbm, hbm, hbm, vmem, vmem],
+        in_specs=[hbm] * 7,
         out_specs=(vmem, vmem) + (hbm,) * len(fresh),
         scratch_shapes=[
+            *[pltpu.VMEM(value.shape, jnp.float32) for value in (block, own_grad, sums, probe_field)],
+            dma((4,)),
             *[pltpu.VMEM(shape.shape, shape.dtype) for shape in shapes],
             pltpu.VMEM(block.shape, jnp.bfloat16),
             pltpu.VMEM(sums.shape, jnp.bfloat16),
@@ -529,8 +591,10 @@
             dma((n_row - 1,)),
             dma((n_row - 1,)),
             dma((n_row - 1,)),
-            dma((n_col - 1,)),
-            dma((n_col - 1,)),
+            dma((n_col // 2,)),
+            dma((n_col // 2,)),
+            dma((n_col // 2,)),
+            dma((n_col // 2,)),
         ],
         compiler_params=pltpu.CompilerParams(
             collective_id=1 if halos else 2,
@@ -550,15 +614,18 @@
     tables = chirp_blocks(frame_size)
     rims = first_halos(object_field, frame_size)
     for iteration in range(ITERS):
+        planes, rows, columns = object_field.shape
         own_grad, *grad_rims, sums = frame_sums(
-            object_field,
+            object_field.reshape(planes, rows // SUBLANES, SUBLANES, columns),
             rims,
             probe_field,
-            amplitudes[iteration],
-            positions[iteration],
-            live_counts[iteration, 0],
+            amplitudes,
+            positions,
+            live_counts,
             tables,
-        )
+            iteration,
+        )
+        own_grad = own_grad.reshape(object_field.shape)
         object_field, probe_field, rims = exchange(
             object_field, own_grad, grad_rims, sums, probe_field, iteration < ITERS - 1
         )

time: 156 us -> 140 us (0.90)
  the two profiles are of different devices: /device:TPU:0 before, /device:TPU:5 now
where the time goes in v2:
time: 140 us; the launch traced here: 137 us
  Pallas kernels  132 us (94%)
  local copies, waits for them, and re-layouts  5.25 us (4%)
    pallas_call x2, Pallas kernels, exchange(): pl.pallas_call(functools.partial(exchange_kernel, n_row, n_col, halos), o...  104 us
    pallas_call x2, Pallas kernels, frame_sums(): pl.pallas_call(functools.partial(frames_kernel, iteration), out_shape=(ja...  16.9 us
    pallas_call x1, Pallas kernels, first_halos(): pl.pallas_call(functools.partial(halo_kernel, n_row, n_col), out_shape=ri...  11 us
    unnamed x17, local copies, waits for them, and re-layouts  5.25 us

profile of v2, /device:TPU:5, one launch (start us, length us, event | category | flops | bytes accessed | tf_op | source)
XLA Modules:
  0.0 137.5 jit_solution(11235065185977367322)
XLA Ops:
  0.6 0.0 copy-start.4
  0.6 0.7 copy.9.live
  1.4 0.0 copy-start
  1.4 1.4 %copy-done = f32[2,512,384]{2,1,0:T(8,128)S(1)} copy-done((f32[2,512,384]{2,1,0:T(8,128)S(1)}, f32[2,512,384]{2,1,0:T(8,128)}, u32[]{:S(2)}) %copy-start) | copy-done | bytes 1572888
  2.8 0.0 copy-start.3
  2.8 0.0 copy-start.5
  2.8 0.0 copy-start.6
  2.8 11.0 %first_halos.1 = (bf16[2,256,384]{2,1,0:T(8,128)(2,1)S(1)}, bf16[2,512,256]{2,1,0:T(8,128)(2,1)S(1)}, bf16[2,256,256]{2,1,0:T(8,128)(2,1)S(1)}) custom-call(f32[2,512,384]{2,1,0:T(8,128)S(1)} %copy-done), custom_call_target="tpu_custom_call" | custom-call | flops 393216 | bytes 4194304 | tf_op jit(solution)/shard_map/first_halos/pallas_call | solution.py:338
  13.9 0.0 copy-done.4
  13.9 0.0 copy-done.3
  13.9 0.0 copy-done.5
  13.9 0.0 copy-done.6
  13.9 6.9 %frames.2 = (f32[2,64,8,384]{3,2,1,0:T(8,128)}, bf16[2,256,384]{2,1,0:T(8,128)(2,1)S(1)}, bf16[2,512,256]{2,1,0:T(8,128)(2,1)S(1)}, bf16[2,256,256]{2,1,0:T(8,128)(2,1)S(1)}, f32[6,256,128]{2,1,0:T(8,128)S(1)}) custom-call(s32[2,2,12]{2,1,0:T(2,128)S(1)} %copy-done.4, s32[2,1,1]{2,1,0:T(1,128)S(1)} %copy.9.live, f32[2,64,8,384]{3,2,1,0:T(8,128)} %bitcast.4, ...), custom_call_target="tpu_custom_call" | custom-call | flops 6442450944 | bytes 12582912 | tf_op jit(solution)/shard_map/frames/pallas_call | solution.py:225
  20.8 51.6 %exchange.2 = (f32[2,512,384]{2,1,0:T(8,128)S(1)}, f32[2,256,256]{2,1,0:T(8,128)S(1)}, bf16[2,256,384]{2,1,0:T(8,128)(2,1)S(1)}, bf16[2,512,256]{2,1,0:T(8,128)(2,1)S(1)}, bf16[2,256,256]{2,1,0:T(8,128)(2,1)S(1)}) custom-call(f32[2,512,384]{2,1,0:T(8,128)} %refs_0_.1, f32[2,512,384]{2,1,0:T(8,128)} %bitcast.7, ...), custom_call_target="tpu_custom_call" | custom-call | flops 786432 | bytes 8388608 | tf_op jit(solution)/shard_map/exchange/pallas_call | solution.py:562
  72.5 0.0 copy-start.1
  72.5 1.1 copy-done.1
  73.6 0.0 copy-start.2
  73.6 9.9 %frames.3 = (f32[2,64,8,384]{3,2,1,0:T(8,128)}, bf16[2,256,384]{2,1,0:T(8,128)(2,1)S(1)}, bf16[2,512,256]{2,1,0:T(8,128)(2,1)S(1)}, bf16[2,256,256]{2,1,0:T(8,128)(2,1)S(1)}, f32[6,256,128]{2,1,0:T(8,128)S(1)}) custom-call(s32[2,2,12]{2,1,0:T(2,128)S(1)} %copy-done.4, s32[2,1,1]{2,1,0:T(1,128)S(1)} %copy.9.live, f32[2,64,8,384]{3,2,1,0:T(8,128)} %bitcast.5, ...), custom_call_target="tpu_custom_call" | custom-call | flops 6442450944 | bytes 12582912 | tf_op jit(solution)/shard_map/frames/pallas_call | solution.py:225
  83.6 0.0 copy-done.2
  83.6 52.0 %exchange.3 = (f32[2,512,384]{2,1,0:T(8,128)S(1)}, f32[2,256,256]{2,1,0:T(8,128)S(1)}) custom-call(f32[2,512,384]{2,1,0:T(8,128)S(1)} %copy-done.2, f32[2,512,384]{2,1,0:T(8,128)} %bitcast.6, bf16[2,256,384]{2,1,0:T(8,128)(2,1)S(1)} %get-tuple-element.34.refs_2_, bf16[2,512,256]{2,1,0:T(8,128)(2,1)S(1)} %get-tuple-element.35.refs_3_, ...), custom_call_target="tpu_custom_call" | custom-call | flops 786432 | bytes 8388608 | tf_op jit(solution)/shard_map/exchange/pallas_call | solution.py:562
  135.5 1.1 copy.13
  136.7 0.8 copy.14
Async XLA Ops:
  0.6 13.2 %copy-start.4 = (s32[2,2,12]{2,1,0:T(2,128)S(1)}, s32[2,2,12]{2,1,0:T(2,128)}, u32[]{:S(2)}) copy-start(s32[2,2,12]{2,1,0:T(2,128)} %positions.3) | copy-start | bytes 580
  1.4 1.4 %copy-start = (f32[2,512,384]{2,1,0:T(8,128)S(1)}, f32[2,512,384]{2,1,0:T(8,128)}, u32[]{:S(2)}) copy-start(f32[2,512,384]{2,1,0:T(8,128)} %refs_0_.1) | copy-start | bytes 4718596
  2.8 11.1 %copy-start.3 = (f32[2,256,256]{2,1,0:T(8,128)S(1)}, f32[2,256,256]{2,1,0:T(8,128)}, u32[]{:S(2)}) copy-start(f32[2,256,256]{2,1,0:T(8,128)} %refs_6_.1) | copy-start | bytes 1572868
  2.8 11.1 %copy-start.5 = (bf16[512,512]{1,0:T(8,128)(2,1)S(1)}, bf16[512,512]{1,0:T(8,128)(2,1)}, u32[]{:S(2)}) copy-start(bf16[512,512]{1,0:T(8,128)(2,1)} %constant.5.clone.right_hbm) | copy-start | bytes 1572868
  2.8 11.1 %copy-start.6 = (bf16[512,512]{1,0:T(8,128)(2,1)S(1)}, bf16[512,512]{1,0:T(8,128)(2,1)}, u32[]{:S(2)}) copy-start(bf16[512,512]{1,0:T(8,128)(2,1)} %constant.4.clone.left_hbm) | copy-start | bytes 1572868
  72.5 1.1 copy-start.1
  73.6 10.0 %copy-start.2 = (f32[2,512,384]{2,1,0:T(8,128)S(1)}, f32[2,512,384]{2,1,0:T(8,128)}, u32[]{:S(2)}) copy-start(f32[2,512,384]{2,1,0:T(8,128)} %copy-done.1) | copy-start | bytes 4718596

commit v3 on v2

--- a/solution.py
+++ b/solution.py
@@ -104,7 +104,7 @@
     def dot(a, b):
         return jnp.dot(a, b, preferred_element_type=jnp.float32)
 
-    def one_frame(slot, weight):
+    def one_frame(slot, weight=None):
         top = positions[iteration, 0, slot]
         left = positions[iteration, 1, slot]
         column_block = left // LANES
@@ -146,8 +146,11 @@
             ],
             axis=0,
         ).astype(jnp.bfloat16)
+        yield
         near = dot(left_table[...], wave).astype(jnp.bfloat16)
+        yield
         far = dot(jnp.concatenate([near[:size], near[size:]], axis=1), right_table[...])
+        yield
         far_real, far_imag = far[:, :size], far[:, size:]
         power = far_real * far_real + far_imag * far_imag
         factor = 1.0 - amplitudes[slot].astype(jnp.float32) * lax.rsqrt(
@@ -156,13 +159,20 @@
         misfit = jnp.concatenate([far_real * factor, far_imag * factor], axis=0).astype(
             jnp.bfloat16
         )
+        yield
         back = dot(right_table[...], misfit).astype(jnp.bfloat16)
+        yield
         update = dot(jnp.concatenate([back[:size], back[size:]], axis=1), left_table[...])
-        update_real, update_imag = update[:, :size] * weight, update[:, size:] * weight
+        yield
+        update_real, update_imag = update[:, :size], update[:, size:]
+        density = patch_real * patch_real + patch_imag * patch_imag
+        if weight is not None:
+            update_real, update_imag = update_real * weight, update_imag * weight
+            density = density * weight
         terms = (
             patch_real * update_real + patch_imag * update_imag,
             patch_real * update_imag - patch_imag * update_real,
-            (patch_real * patch_real + patch_imag * patch_imag) * weight,
+            density,
         )
         for comp, term in enumerate(terms):
             for half in range(halves):
@@ -202,8 +212,12 @@
     count = live[iteration, 0, 0]
 
     def pair(index, carry):
-        one_frame(2 * index, jnp.float32(1.0))
-        one_frame(2 * index + 1, (2 * index + 1 < count).astype(jnp.float32))
+        second_weight = (2 * index + 1 < count).astype(jnp.float32)
+        leading = one_frame(2 * index)
+        lagging = one_frame(2 * index + 1, second_weight)
+        next(leading)
+        for running in (leading, lagging) * 7:
+            next(running, None)
         return carry
 
     lax.fori_loop(0, (count + 1) // 2, pair, 0)
@@ -270,7 +284,6 @@
         return (
             (self.above, (row - 1, col)),
             (self.left, (row, col - 1)),
-            (jnp.logical_and(self.above, self.left), (row - 1, col - 1)),
         )
 
     def ahead(self):
@@ -278,7 +291,6 @@
         return (
             (self.under, (row + 1, col)),
             (self.right, (row, col + 1)),
-            (jnp.logical_and(self.under, self.right), (row + 1, col + 1)),
         )
 
 
@@ -291,26 +303,37 @@
 
 
 def send_halos(near, narrow, rims, send, recv):
-    _, height, _ = rims[0].shape
-    _, _, width = rims[1].shape
-    sources = (
-        narrow.at[:, :height, :],
-        narrow.at[:, :, :width],
-        narrow.at[:, :height, :width],
-    )
-    sent = []
-    for index, (there, device) in enumerate(near.back()):
-        copy = remote(sources[index], rims[index], send.at[index], recv.at[index], device)
+    below, beside, corner = rims
+    _, height, size = corner.shape
+    (above, up), (left, aside) = near.back()
+    (under, _), (right, _) = near.ahead()
+    first, rest = slice(0, size), slice(size, None)
+    pieces = (
+        (narrow.at[:, :height, first], below.at[:, :, first], up),
+        (narrow.at[:, :height, rest], below.at[:, :, rest], up),
+        (narrow.at[:, :, first], beside, aside),
+        (below.at[:, :, first], corner, aside),
+    )
+    sent = [
+        remote(source, target, send.at[index], recv.at[index], device)
+        for index, (source, target, device) in enumerate(pieces)
+    ]
+    relays = jnp.logical_and(under, left)
+    relayed = jnp.logical_and(under, right)
+    for copy, there in zip(sent, (above, above, left)):
         pl.when(there)(copy.start)
-        sent.append(copy)
+
+    def relay():
+        pl.when(under)(sent[0].wait_recv)
+        pl.when(relays)(sent[3].start)
 
     def finish():
-        for copy, (there, _) in zip(sent, near.ahead()):
+        for copy, there in zip(sent[1:], (under, right, relayed)):
             pl.when(there)(copy.wait_recv)
-        for copy, (there, _) in zip(sent, near.back()):
+        for copy, there in zip(sent, (above, above, left, relays)):
             pl.when(there)(copy.wait_send)
 
-    return finish
+    return relay, finish
 
 
 def halo_kernel(n_row, n_col, block, below, beside, corner, narrow, send, recv):
@@ -320,7 +343,9 @@
         pl.when(there)(functools.partial(greet, barrier, device))
     narrow[...] = block[...].astype(jnp.bfloat16)
     pl.semaphore_wait(barrier, how_many(near.back() + near.ahead()))
-    send_halos(near, narrow, (below, beside, corner), send, recv)()
+    relay, finish = send_halos(near, narrow, (below, beside, corner), send, recv)
+    relay()
+    finish()
 
 
 def rim_shapes(block, size):
@@ -340,7 +365,7 @@
         out_shape=rim_shapes(block, size),
         in_specs=[pl.BlockSpec(memory_space=pltpu.VMEM)],
         out_specs=(hbm,) * 3,
-        scratch_shapes=[pltpu.VMEM(block.shape, jnp.bfloat16), dma((3,)), dma((3,))],
+        scratch_shapes=[pltpu.VMEM(block.shape, jnp.bfloat16), dma((4,)), dma((4,))],
         compiler_params=pltpu.CompilerParams(
             collective_id=0, has_side_effects=True, vmem_limit_bytes=32 * 1024 * 1024
         ),
@@ -377,6 +402,7 @@
         steps,
         joined,
         got_steps,
+        mixed,
         grad_send,
         grad_recv,
         halo_send,
@@ -395,7 +421,13 @@
     loads = [
         local_copy(source, target, load.at[index])
         for index, (source, target) in enumerate(
-            ((sums_hbm, sums), (probe_hbm, probe), (block_hbm, block), (own_grad_hbm, own_grad))
+            (
+                (sums_hbm, sums),
+                (probe_hbm, probe),
+                (block_hbm, block),
+                (own_grad_hbm, own_grad),
+                (below_grad.at[:, :, : mixed.shape[2]], mixed),
+            )
         )
     ]
     near = Neighbours(n_row, n_col)
@@ -417,12 +449,9 @@
         greet(barrier, along_col(step))
     for step in range(1, n_row):
         greet(barrier, along_row(step))
-    corners = (near.back()[2], near.ahead()[2])
-    for there, device in corners:
-        pl.when(there)(functools.partial(greet, barrier, device))
     loads[0].wait()
     wide[...] = sums[...].astype(jnp.bfloat16)
-    pl.semaphore_wait(barrier, n_col + n_row - 2 + how_many(corners))
+    pl.semaphore_wait(barrier, n_col + n_row - 2)
 
     def started(source, target, send, recv, device):
         copy = remote(source, target, send, recv, device)
@@ -444,13 +473,23 @@
                 along_col(step),
             )
         )
-    grads = []
-    pairs = ((below_grad, got_below), (beside_grad, got_beside), (corner_grad, got_corner))
-    for index, (there, device) in enumerate(near.ahead()):
-        source, target = pairs[index]
-        copy = remote(source, target, grad_send.at[index], grad_recv.at[index], device)
-        pl.when(there)(copy.start)
-        grads.append(copy)
+    (above, _), (left, _) = near.back()
+    (under, down), (right, aside) = near.ahead()
+    started_corner = jnp.logical_and(under, right)
+    got_corner_here = jnp.logical_and(under, left)
+    width = size
+    pieces = (
+        (corner_grad, got_corner, aside, started_corner, got_corner_here),
+        (below_grad.at[:, :, width:], got_below.at[:, :, width:], down, under, above),
+        (beside_grad, got_beside, aside, right, left),
+        (mixed, got_below.at[:, :, :width], down, under, above),
+    )
+    grads = [
+        remote(source, target, grad_send.at[index], grad_recv.at[index], device)
+        for index, (source, target, device, _, _) in enumerate(pieces)
+    ]
+    for copy, piece_of in zip(grads[:3], pieces):
+        pl.when(piece_of[3])(copy.start)
     for copy in loads[1:]:
         copy.wait()
     step_size = ALPHA / (jnp.max(probe[0] * probe[0] + probe[1] * probe[1]) + 1e-06)
@@ -475,6 +514,14 @@
             )
         )
 
+    def mix_corner():
+        grads[0].wait_recv()
+        mixed[...] = (
+            mixed[...].astype(jnp.float32) + got_corner[...].astype(jnp.float32)
+        ).astype(jnp.bfloat16)
+
+    pl.when(got_corner_here)(mix_corner)
+    pl.when(under)(grads[3].start)
     total = own_rows[row]
     for step, copy in enumerate(second):
         copy.wait_recv()
@@ -513,25 +560,28 @@
     ]
     over = [started(joined, got_steps.at[col], core_send.at[0], core_recv.at[0], other)]
 
-    for index, (there, _) in enumerate(near.back()):
-        target = pairs[index][1]
-        copy = grads[index]
-        _, height, width = target.shape
-
-        def add_rim():
-            copy.wait_recv()
-            new_block[:, :height, :width] -= step_size * target[...].astype(jnp.float32)
-
-        pl.when(there)(add_rim)
+    def add_below():
+        grads[1].wait_recv()
+        grads[3].wait_recv()
+        new_block[:, :size, :] -= step_size * got_below[...].astype(jnp.float32)
+
+    def add_beside():
+        grads[2].wait_recv()
+        new_block[:, :, :size] -= step_size * got_beside[...].astype(jnp.float32)
+
+    pl.when(above)(add_below)
+    pl.when(left)(add_beside)
     if halos:
         narrow[...] = new_block[...].astype(jnp.bfloat16)
-        finish_halos = send_halos(near, narrow, rims, halo_send, halo_recv)
+        relay_halos, finish_halos = send_halos(near, narrow, rims, halo_send, halo_recv)
 
 
     for step in range(1, count):
         across[step - 1].wait_recv()
         slot = got_steps.at[lax.rem(place + count - step, count) * 2 + core]
         over.append(started(slot, slot, core_send.at[step], core_recv.at[step], other))
+    if halos:
+        relay_halos()
     for copy in over:
         copy.wait_recv()
     for index in range(n_col):
@@ -542,8 +592,8 @@
             out[comp, rows, lanes] = probe[comp, rows, lanes] - got_steps[index, plane]
     for copy in first + second + third + across + over:
         copy.wait_send()
-    for copy, (there, _) in zip(grads, near.ahead()):
-        pl.when(there)(copy.wait_send)
+    for copy, piece_of in zip(grads, pieces):
+        pl.when(piece_of[3])(copy.wait_send)
     if halos:
         finish_halos()
 
@@ -570,7 +620,7 @@
         out_specs=(vmem, vmem) + (hbm,) * len(fresh),
         scratch_shapes=[
             *[pltpu.VMEM(value.shape, jnp.float32) for value in (block, own_grad, sums, probe_field)],
-            dma((4,)),
+            dma((5,)),
             *[pltpu.VMEM(shape.shape, shape.dtype) for shape in shapes],
             pltpu.VMEM(block.shape, jnp.bfloat16),
             pltpu.VMEM(sums.shape, jnp.bfloat16),
@@ -581,10 +631,8 @@
             pltpu.VMEM((n_row, comps, part, LANES), jnp.float32),
             pltpu.VMEM((comps, chunk, LANES), jnp.float32),
             pltpu.VMEM((n_col, comps, chunk, LANES), jnp.float32),
-            dma((3,)),
-            dma((3,)),
-            dma((3,)),
-            dma((3,)),
+            pltpu.VMEM(shapes[2].shape, shapes[2].dtype),
+            *[dma((4,))] * 4,
             dma((n_col - 1,)),
             dma((n_col - 1,)),
             dma((n_row - 1,)),

time: 140 us -> 117 us (0.84)
  the two profiles are of different devices: /device:TPU:5 before, /device:TPU:25 now
where the time goes in v3:
time: 117 us
  Pallas kernels  111 us (95%)
  local copies, waits for them, and re-layouts  5.25 us (4%)
    pallas_call x2, Pallas kernels, exchange(): pl.pallas_call(functools.partial(exchange_kernel, n_row, n_col, halos), o...  83.8 us
    pallas_call x1, Pallas kernels, first_halos(): pl.pallas_call(functools.partial(halo_kernel, n_row, n_col), out_shape=ri...  15.1 us
    pallas_call x2, Pallas kernels, frame_sums(): pl.pallas_call(functools.partial(frames_kernel, iteration), out_shape=(ja...  12.6 us
    unnamed x17, local copies, waits for them, and re-layouts  5.25 us

profile of v3, /device:TPU:25, one launch (start us, length us, event | category | flops | bytes accessed | tf_op | source)
XLA Modules:
  0.0 117.4 jit_solution(14818184428358304032)
XLA Ops:
  0.6 0.0 copy-start.4
  0.6 0.7 copy.9.live
  1.4 0.0 copy-start
  1.4 1.4 %copy-done = f32[2,512,384]{2,1,0:T(8,128)S(1)} copy-done((f32[2,512,384]{2,1,0:T(8,128)S(1)}, f32[2,512,384]{2,1,0:T(8,128)}, u32[]{:S(2)}) %copy-start) | copy-done | bytes 1572888
  2.8 0.0 copy-start.3
  2.8 0.0 copy-start.5
  2.8 0.0 copy-start.6
  2.8 15.1 %first_halos.1 = (bf16[2,256,384]{2,1,0:T(8,128)(2,1)S(1)}, bf16[2,512,256]{2,1,0:T(8,128)(2,1)S(1)}, bf16[2,256,256]{2,1,0:T(8,128)(2,1)S(1)}) custom-call(f32[2,512,384]{2,1,0:T(8,128)S(1)} %copy-done), custom_call_target="tpu_custom_call" | custom-call | flops 393216 | bytes 4194304 | tf_op jit(solution)/shard_map/first_halos/pallas_call | solution.py:363
  17.9 0.0 copy-done.4
  17.9 0.0 copy-done.3
  17.9 0.0 copy-done.5
  17.9 0.0 copy-done.6
  17.9 6.3 %frames.2 = (f32[2,64,8,384]{3,2,1,0:T(8,128)}, bf16[2,256,384]{2,1,0:T(8,128)(2,1)S(1)}, bf16[2,512,256]{2,1,0:T(8,128)(2,1)S(1)}, bf16[2,256,256]{2,1,0:T(8,128)(2,1)S(1)}, f32[6,256,128]{2,1,0:T(8,128)S(1)}) custom-call(s32[2,2,12]{2,1,0:T(2,128)S(1)} %copy-done.4, s32[2,1,1]{2,1,0:T(1,128)S(1)} %copy.9.live, f32[2,64,8,384]{3,2,1,0:T(8,128)} %bitcast.4, ...), custom_call_target="tpu_custom_call" | custom-call | flops 6442450944 | bytes 12582912 | tf_op jit(solution)/shard_map/frames/pallas_call | solution.py:239
  24.2 44.9 %exchange.2 = (f32[2,512,384]{2,1,0:T(8,128)S(1)}, f32[2,256,256]{2,1,0:T(8,128)S(1)}, bf16[2,256,384]{2,1,0:T(8,128)(2,1)S(1)}, bf16[2,512,256]{2,1,0:T(8,128)(2,1)S(1)}, bf16[2,256,256]{2,1,0:T(8,128)(2,1)S(1)}) custom-call(f32[2,512,384]{2,1,0:T(8,128)} %refs_0_.1, f32[2,512,384]{2,1,0:T(8,128)} %bitcast.7, ...), custom_call_target="tpu_custom_call" | custom-call | flops 786432 | bytes 8388608 | tf_op jit(solution)/shard_map/exchange/pallas_call | solution.py:612
  69.1 0.0 copy-start.1
  69.1 1.1 copy-done.1
  70.2 0.0 copy-start.2
  70.2 6.3 %frames.3 = (f32[2,64,8,384]{3,2,1,0:T(8,128)}, bf16[2,256,384]{2,1,0:T(8,128)(2,1)S(1)}, bf16[2,512,256]{2,1,0:T(8,128)(2,1)S(1)}, bf16[2,256,256]{2,1,0:T(8,128)(2,1)S(1)}, f32[6,256,128]{2,1,0:T(8,128)S(1)}) custom-call(s32[2,2,12]{2,1,0:T(2,128)S(1)} %copy-done.4, s32[2,1,1]{2,1,0:T(1,128)S(1)} %copy.9.live, f32[2,64,8,384]{3,2,1,0:T(8,128)} %bitcast.5, ...), custom_call_target="tpu_custom_call" | custom-call | flops 6442450944 | bytes 12582912 | tf_op jit(solution)/shard_map/frames/pallas_call | solution.py:239
  76.5 0.0 copy-done.2
  76.5 38.9 %exchange.3 = (f32[2,512,384]{2,1,0:T(8,128)S(1)}, f32[2,256,256]{2,1,0:T(8,128)S(1)}) custom-call(f32[2,512,384]{2,1,0:T(8,128)S(1)} %copy-done.2, f32[2,512,384]{2,1,0:T(8,128)} %bitcast.6, bf16[2,256,384]{2,1,0:T(8,128)(2,1)S(1)} %get-tuple-element.34.refs_2_, bf16[2,512,256]{2,1,0:T(8,128)(2,1)S(1)} %get-tuple-element.35.refs_3_, ...), custom_call_target="tpu_custom_call" | custom-call | flops 786432 | bytes 8388608 | tf_op jit(solution)/shard_map/exchange/pallas_call | solution.py:612
  115.4 1.1 copy.13
  116.6 0.8 copy.14
Async XLA Ops:
  0.6 17.2 %copy-start.4 = (s32[2,2,12]{2,1,0:T(2,128)S(1)}, s32[2,2,12]{2,1,0:T(2,128)}, u32[]{:S(2)}) copy-start(s32[2,2,12]{2,1,0:T(2,128)} %positions.3) | copy-start | bytes 580
  1.4 1.4 %copy-start = (f32[2,512,384]{2,1,0:T(8,128)S(1)}, f32[2,512,384]{2,1,0:T(8,128)}, u32[]{:S(2)}) copy-start(f32[2,512,384]{2,1,0:T(8,128)} %refs_0_.1) | copy-start | bytes 4718596
  2.8 15.1 %copy-start.3 = (f32[2,256,256]{2,1,0:T(8,128)S(1)}, f32[2,256,256]{2,1,0:T(8,128)}, u32[]{:S(2)}) copy-start(f32[2,256,256]{2,1,0:T(8,128)} %refs_6_.1) | copy-start | bytes 1572868
  2.8 15.1 %copy-start.5 = (bf16[512,512]{1,0:T(8,128)(2,1)S(1)}, bf16[512,512]{1,0:T(8,128)(2,1)}, u32[]{:S(2)}) copy-start(bf16[512,512]{1,0:T(8,128)(2,1)} %constant.5.clone.right_hbm) | copy-start | bytes 1572868
  2.8 15.1 %copy-start.6 = (bf16[512,512]{1,0:T(8,128)(2,1)S(1)}, bf16[512,512]{1,0:T(8,128)(2,1)}, u32[]{:S(2)}) copy-start(bf16[512,512]{1,0:T(8,128)(2,1)} %constant.4.clone.left_hbm) | copy-start | bytes 1572868
  69.1 1.1 copy-start.1
  70.2 6.3 %copy-start.2 = (f32[2,512,384]{2,1,0:T(8,128)S(1)}, f32[2,512,384]{2,1,0:T(8,128)}, u32[]{:S(2)}) copy-start(f32[2,512,384]{2,1,0:T(8,128)} %copy-done.1) | copy-start | bytes 4718596

commit v4 on v3

--- a/solution.py
+++ b/solution.py
@@ -17,6 +17,8 @@
 ALPHA = 0.5
 LANES = 128
 SUBLANES = 8
+TOGETHER = 4
+STAGES = 7
 MESH = pl.DeviceIdType.MESH
 
 
@@ -211,16 +213,18 @@
 
     count = live[iteration, 0, 0]
 
-    def pair(index, carry):
-        second_weight = (2 * index + 1 < count).astype(jnp.float32)
-        leading = one_frame(2 * index)
-        lagging = one_frame(2 * index + 1, second_weight)
-        next(leading)
-        for running in (leading, lagging) * 7:
-            next(running, None)
+    def together(index, carry):
+        first = TOGETHER * index
+        running = [one_frame(first)] + [
+            one_frame(first + later, (first + later < count).astype(jnp.float32))
+            for later in range(1, TOGETHER)
+        ]
+        for step in range(STAGES + TOGETHER - 1):
+            for frame in running[: step + 1]:
+                next(frame, None)
         return carry
 
-    lax.fori_loop(0, (count + 1) // 2, pair, 0)
+    lax.fori_loop(0, (count + TOGETHER - 1) // TOGETHER, together, 0)
     leaving = local_copy(gathered.at[inner], own_grad, semaphores.at[0])
     for _, target, groups, lanes in regions:
         target[...] = gathered[:, groups, :, lanes].reshape(target.shape).astype(target.dtype)
@@ -243,8 +247,8 @@
             *[jax.ShapeDtypeStruct(rim.shape, jnp.bfloat16) for rim in rims],
             jax.ShapeDtypeStruct((3 * size // LANES, size, LANES), jnp.float32),
         ),
-        in_specs=[smem, smem] + [hbm] * 8,
-        out_specs=(hbm,) + (vmem,) * 4,
+        in_specs=[smem, smem, vmem] + [hbm] * 7,
+        out_specs=(vmem,) * 5,
         scratch_shapes=[
             pltpu.VMEM(whole, jnp.float32),
             pltpu.VMEM(whole, jnp.float32),
@@ -302,7 +306,7 @@
     return sum(there.astype(jnp.int32) for there, _ in neighbours)
 
 
-def send_halos(near, narrow, rims, send, recv):
+def send_halos(near, narrow, rims, send, recv, prepare):
     below, beside, corner = rims
     _, height, size = corner.shape
     (above, up), (left, aside) = near.back()
@@ -320,8 +324,10 @@
     ]
     relays = jnp.logical_and(under, left)
     relayed = jnp.logical_and(under, right)
-    for copy, there in zip(sent, (above, above, left)):
-        pl.when(there)(copy.start)
+    for copy in sent[:2]:
+        pl.when(above)(copy.start)
+    prepare()
+    pl.when(left)(sent[2].start)
 
     def relay():
         pl.when(under)(sent[0].wait_recv)
@@ -336,14 +342,28 @@
     return relay, finish
 
 
-def halo_kernel(n_row, n_col, block, below, beside, corner, narrow, send, recv):
+def halo_kernel(
+    n_row, n_col, block_hbm, below, beside, corner, block, narrow, load, send, recv
+):
+    _, height, size = corner.shape
+    parts = (slice(0, height), slice(height, None))
+    loads = [
+        local_copy(block_hbm.at[:, rows], block.at[:, rows], load.at[index])
+        for index, rows in enumerate(parts)
+    ]
     near = Neighbours(n_row, n_col)
     barrier = pltpu.get_barrier_semaphore()
     for there, device in near.back() + near.ahead():
         pl.when(there)(functools.partial(greet, barrier, device))
-    narrow[...] = block[...].astype(jnp.bfloat16)
+    loads[0].wait()
+    narrow[:, parts[0]] = block[:, parts[0]].astype(jnp.bfloat16)
     pl.semaphore_wait(barrier, how_many(near.back() + near.ahead()))
-    relay, finish = send_halos(near, narrow, (below, beside, corner), send, recv)
+
+    def rest():
+        loads[1].wait()
+        narrow[:, parts[1]] = block[:, parts[1]].astype(jnp.bfloat16)
+
+    relay, finish = send_halos(near, narrow, (below, beside, corner), send, recv, rest)
     relay()
     finish()
 
@@ -363,9 +383,15 @@
     return pl.pallas_call(
         functools.partial(halo_kernel, n_row, n_col),
         out_shape=rim_shapes(block, size),
-        in_specs=[pl.BlockSpec(memory_space=pltpu.VMEM)],
+        in_specs=[hbm],
         out_specs=(hbm,) * 3,
-        scratch_shapes=[pltpu.VMEM(block.shape, jnp.bfloat16), dma((4,)), dma((4,))],
+        scratch_shapes=[
+            pltpu.VMEM(block.shape, jnp.float32),
+            pltpu.VMEM(block.shape, jnp.bfloat16),
+            dma((2,)),
+            dma((4,)),
+            dma((4,)),
+        ],
         compiler_params=pltpu.CompilerParams(
             collective_id=0, has_side_effects=True, vmem_limit_bytes=32 * 1024 * 1024
         ),
@@ -488,7 +514,7 @@
         remote(source, target, grad_send.at[index], grad_recv.at[index], device)
         for index, (source, target, device, _, _) in enumerate(pieces)
     ]
-    for copy, piece_of in zip(grads[:3], pieces):
+    for copy, piece_of in zip(grads[:2], pieces):
         pl.when(piece_of[3])(copy.start)
     for copy in loads[1:]:
         copy.wait()
@@ -514,6 +540,8 @@
             )
         )
 
+    pl.when(right)(grads[2].start)
+
     def mix_corner():
         grads[0].wait_recv()
         mixed[...] = (
@@ -569,12 +597,15 @@
         grads[2].wait_recv()
         new_block[:, :, :size] -= step_size * got_beside[...].astype(jnp.float32)
 
-    pl.when(above)(add_below)
     pl.when(left)(add_beside)
     if halos:
-        narrow[...] = new_block[...].astype(jnp.bfloat16)
-        relay_halos, finish_halos = send_halos(near, narrow, rims, halo_send, halo_recv)
-
+        narrow[:, size:] = new_block[:, size:].astype(jnp.bfloat16)
+    pl.when(above)(add_below)
+    if halos:
+        narrow[:, :size] = new_block[:, :size].astype(jnp.bfloat16)
+        relay_halos, finish_halos = send_halos(
+            near, narrow, rims, halo_send, halo_recv, lambda: None
+        )
 
     for step in range(1, count):
         across[step - 1].wait_recv()

time: 117 us -> 116 us (level); the launches traced: 117 us -> 114 us
  Pallas kernels: 111 us -> 108 us
    pallas_call x2, Pallas kernels: 83.8 us -> 75.1 us  [exchange(): pl.pallas_call(functools.partial(exchange_kernel, n_row, n_col, halos), o...]
    pallas_call x2, Pallas kernels: 12.6 us -> 17.6 us  [frame_sums(): pl.pallas_call(functools.partial(frames_kernel, iteration), out_shape=(ja...]
where the time goes in v4:
time: 116 us; the launch traced here: 114 us
  Pallas kernels  108 us (93%)
  local copies, waits for them, and re-layouts  5.25 us (5%)
    pallas_call x2, Pallas kernels, exchange(): pl.pallas_call(functools.partial(exchange_kernel, n_row, n_col, halos), o...  75.1 us
    pallas_call x2, Pallas kernels, frame_sums(): pl.pallas_call(functools.partial(frames_kernel, iteration), out_shape=(ja...  17.6 us
    pallas_call x1, Pallas kernels, first_halos(): pl.pallas_call(functools.partial(halo_kernel, n_row, n_col), out_shape=ri...  15.2 us
    unnamed x17, local copies, waits for them, and re-layouts  5.25 us

profile of v4, /device:TPU:25, one launch (start us, length us, event | category | flops | bytes accessed | tf_op | source)
XLA Modules:
  0.0 113.9 jit_solution(7626359747944417393)
XLA Ops:
  0.6 0.0 copy-start.4
  0.6 0.7 copy.9.live
  1.4 0.0 copy-start
  1.4 1.4 %copy-done = f32[2,512,384]{2,1,0:T(8,128)S(1)} copy-done((f32[2,512,384]{2,1,0:T(8,128)S(1)}, f32[2,512,384]{2,1,0:T(8,128)}, u32[]{:S(2)}) %copy-start) | copy-done | bytes 1572888
  2.8 0.0 copy-start.3
  2.8 0.0 copy-start.5
  2.8 0.0 copy-start.6
  2.8 15.2 %first_halos.1 = (bf16[2,256,384]{2,1,0:T(8,128)(2,1)S(1)}, bf16[2,512,256]{2,1,0:T(8,128)(2,1)S(1)}, bf16[2,256,256]{2,1,0:T(8,128)(2,1)S(1)}) custom-call(f32[2,512,384]{2,1,0:T(8,128)S(1)} %copy-done), custom_call_target="tpu_custom_call" | custom-call | flops 393216 | bytes 4194304 | tf_op jit(solution)/shard_map/first_halos/pallas_call | solution.py:383
  18.0 0.0 copy-done.4
  18.0 0.0 copy-done.3
  18.0 0.0 copy-done.5
  18.1 0.0 copy-done.6
  18.1 8.7 %frames.2 = (f32[2,64,8,384]{3,2,1,0:T(8,128)}, bf16[2,256,384]{2,1,0:T(8,128)(2,1)S(1)}, bf16[2,512,256]{2,1,0:T(8,128)(2,1)S(1)}, bf16[2,256,256]{2,1,0:T(8,128)(2,1)S(1)}, f32[6,256,128]{2,1,0:T(8,128)S(1)}) custom-call(s32[2,2,12]{2,1,0:T(2,128)S(1)} %copy-done.4, s32[2,1,1]{2,1,0:T(1,128)S(1)} %copy.9.live, f32[2,64,8,384]{3,2,1,0:T(8,128)} %bitcast.4, ...), custom_call_target="tpu_custom_call" | custom-call | flops 6442450944 | bytes 12582912 | tf_op jit(solution)/shard_map/frames/pallas_call | solution.py:243
  26.8 43.1 %exchange.2 = (f32[2,512,384]{2,1,0:T(8,128)S(1)}, f32[2,256,256]{2,1,0:T(8,128)S(1)}, bf16[2,256,384]{2,1,0:T(8,128)(2,1)S(1)}, bf16[2,512,256]{2,1,0:T(8,128)(2,1)S(1)}, bf16[2,256,256]{2,1,0:T(8,128)(2,1)S(1)}) custom-call(f32[2,512,384]{2,1,0:T(8,128)} %refs_0_.1, f32[2,512,384]{2,1,0:T(8,128)} %bitcast.7, ...), custom_call_target="tpu_custom_call" | custom-call | flops 786432 | bytes 8388608 | tf_op jit(solution)/shard_map/exchange/pallas_call | solution.py:643
  70.0 0.0 copy-start.1
  70.0 1.1 copy-done.1
  71.1 0.0 copy-start.2
  71.1 8.8 %frames.3 = (f32[2,64,8,384]{3,2,1,0:T(8,128)}, bf16[2,256,384]{2,1,0:T(8,128)(2,1)S(1)}, bf16[2,512,256]{2,1,0:T(8,128)(2,1)S(1)}, bf16[2,256,256]{2,1,0:T(8,128)(2,1)S(1)}, f32[6,256,128]{2,1,0:T(8,128)S(1)}) custom-call(s32[2,2,12]{2,1,0:T(2,128)S(1)} %copy-done.4, s32[2,1,1]{2,1,0:T(1,128)S(1)} %copy.9.live, f32[2,64,8,384]{3,2,1,0:T(8,128)} %bitcast.5, ...), custom_call_target="tpu_custom_call" | custom-call | flops 6442450944 | bytes 12582912 | tf_op jit(solution)/shard_map/frames/pallas_call | solution.py:243
  80.0 0.0 copy-done.2
  80.0 31.9 %exchange.3 = (f32[2,512,384]{2,1,0:T(8,128)S(1)}, f32[2,256,256]{2,1,0:T(8,128)S(1)}) custom-call(f32[2,512,384]{2,1,0:T(8,128)S(1)} %copy-done.2, f32[2,512,384]{2,1,0:T(8,128)} %bitcast.6, bf16[2,256,384]{2,1,0:T(8,128)(2,1)S(1)} %get-tuple-element.34.refs_2_, bf16[2,512,256]{2,1,0:T(8,128)(2,1)S(1)} %get-tuple-element.35.refs_3_, ...), custom_call_target="tpu_custom_call" | custom-call | flops 786432 | bytes 8388608 | tf_op jit(solution)/shard_map/exchange/pallas_call | solution.py:643
  111.9 1.1 %copy.13 = f32[2,512,384]{2,1,0:T(8,128)} copy(f32[2,512,384]{2,1,0:T(8,128)S(1)} %get-tuple-element.40) | data formatting | bytes 3145728
  113.1 0.8 copy.14
Async XLA Ops:
  0.6 17.4 %copy-start.4 = (s32[2,2,12]{2,1,0:T(2,128)S(1)}, s32[2,2,12]{2,1,0:T(2,128)}, u32[]{:S(2)}) copy-start(s32[2,2,12]{2,1,0:T(2,128)} %positions.3) | copy-start | bytes 580
  1.4 1.4 %copy-start = (f32[2,512,384]{2,1,0:T(8,128)S(1)}, f32[2,512,384]{2,1,0:T(8,128)}, u32[]{:S(2)}) copy-start(f32[2,512,384]{2,1,0:T(8,128)} %refs_0_.1) | copy-start | bytes 4718596
  2.8 15.2 %copy-start.3 = (f32[2,256,256]{2,1,0:T(8,128)S(1)}, f32[2,256,256]{2,1,0:T(8,128)}, u32[]{:S(2)}) copy-start(f32[2,256,256]{2,1,0:T(8,128)} %refs_6_.1) | copy-start | bytes 1572868
  2.8 15.3 %copy-start.5 = (bf16[512,512]{1,0:T(8,128)(2,1)S(1)}, bf16[512,512]{1,0:T(8,128)(2,1)}, u32[]{:S(2)}) copy-start(bf16[512,512]{1,0:T(8,128)(2,1)} %constant.5.clone.right_hbm) | copy-start | bytes 1572868
  2.8 15.3 %copy-start.6 = (bf16[512,512]{1,0:T(8,128)(2,1)S(1)}, bf16[512,512]{1,0:T(8,128)(2,1)}, u32[]{:S(2)}) copy-start(bf16[512,512]{1,0:T(8,128)(2,1)} %constant.4.clone.left_hbm) | copy-start | bytes 1572868
  70.0 1.1 %copy-start.1 = (f32[2,512,384]{2,1,0:T(8,128)}, f32[2,512,384]{2,1,0:T(8,128)S(1)}, u32[]{:S(2)}) copy-start(f32[2,512,384]{2,1,0:T(8,128)S(1)} %get-tuple-element.28.refs_0_) | copy-start | bytes 4718596
  71.1 8.9 %copy-start.2 = (f32[2,512,384]{2,1,0:T(8,128)S(1)}, f32[2,512,384]{2,1,0:T(8,128)}, u32[]{:S(2)}) copy-start(f32[2,512,384]{2,1,0:T(8,128)} %copy-done.1) | copy-start | bytes 4718596

commit v5 on v4

--- a/solution.py
+++ b/solution.py
@@ -247,7 +247,7 @@
             *[jax.ShapeDtypeStruct(rim.shape, jnp.bfloat16) for rim in rims],
             jax.ShapeDtypeStruct((3 * size // LANES, size, LANES), jnp.float32),
         ),
-        in_specs=[smem, smem, vmem] + [hbm] * 7,
+        in_specs=[smem, smem] + [hbm] * 8,
         out_specs=(vmem,) * 5,
         scratch_shapes=[
             pltpu.VMEM(whole, jnp.float32),
@@ -383,7 +383,7 @@
     return pl.pallas_call(
         functools.partial(halo_kernel, n_row, n_col),
         out_shape=rim_shapes(block, size),
-        in_specs=[hbm],
+        in_specs=[pl.BlockSpec(memory_space=pltpu.HBM)],
         out_specs=(hbm,) * 3,
         scratch_shapes=[
             pltpu.VMEM(block.shape, jnp.float32),
@@ -403,18 +403,18 @@
 
 
 def exchange_kernel(n_row, n_col, halos, *refs):
-    block_hbm, own_grad_hbm, below_grad, beside_grad, corner_grad, sums_hbm, probe_hbm = refs[:7]
+    block_hbm, own_grad, below_grad, beside_grad, corner_grad, sums, probe = refs[:7]
     refs = refs[7:]
     rims = ()
-    new_block, out = refs[:2]
+    block_out, out = refs[:2]
     refs = refs[2:]
     if halos:
         rims, refs = refs[:3], refs[3:]
+    new_block = block_out
+    if halos:
+        new_block, refs = refs[0], refs[1:]
     (
         block,
-        own_grad,
-        sums,
-        probe,
         load,
         got_below,
         got_beside,
@@ -422,6 +422,7 @@
         narrow,
         wide,
         got_col,
+        kept,
         own_rows,
         got_row,
         piece,
@@ -447,13 +448,7 @@
     loads = [
         local_copy(source, target, load.at[index])
         for index, (source, target) in enumerate(
-            (
-                (sums_hbm, sums),
-                (probe_hbm, probe),
-                (block_hbm, block),
-                (own_grad_hbm, own_grad),
-                (below_grad.at[:, :, : mixed.shape[2]], mixed),
-            )
+            ((block_hbm, block), (below_grad.at[:, :, : mixed.shape[2]], mixed))
         )
     ]
     near = Neighbours(n_row, n_col)
@@ -475,7 +470,6 @@
         greet(barrier, along_col(step))
     for step in range(1, n_row):
         greet(barrier, along_row(step))
-    loads[0].wait()
     wide[...] = sums[...].astype(jnp.bfloat16)
     pl.semaphore_wait(barrier, n_col + n_row - 2)
 
@@ -516,7 +510,7 @@
     ]
     for copy, piece_of in zip(grads[:2], pieces):
         pl.when(piece_of[3])(copy.start)
-    for copy in loads[1:]:
+    for copy in loads:
         copy.wait()
     step_size = ALPHA / (jnp.max(probe[0] * probe[0] + probe[1] * probe[1]) + 1e-06)
     new_block[...] = block[...] - step_size * own_grad[...]
@@ -525,8 +519,14 @@
     for step, copy in enumerate(first):
         copy.wait_recv()
         total = total + got_col[step].astype(jnp.float32)
+    spare = own_rows.shape[1] - planes * part
     for index in range(n_row):
-        own_rows[index] = total[:, index * part : (index + 1) * part, :]
+        rows = slice(index * part, (index + 1) * part)
+        flat = jnp.concatenate([total[plane, rows] for plane in range(planes)], axis=0)
+        kept[index] = flat
+        if spare:
+            flat = jnp.concatenate([flat, jnp.zeros((spare, LANES), jnp.float32)], axis=0)
+        own_rows[index] = flat.astype(jnp.bfloat16)
     second = []
     for step in range(1, n_row):
         their = lax.rem(row + step, n_row)
@@ -550,13 +550,14 @@
 
     pl.when(got_corner_here)(mix_corner)
     pl.when(under)(grads[3].start)
-    total = own_rows[row]
+    total = kept[row]
     for step, copy in enumerate(second):
         copy.wait_recv()
-        total = total + got_row[step]
-    weight = total[2 * halves :] + 1.0
+        total = total + got_row[step].astype(jnp.float32)[: planes * part]
+    third_part = halves * part
+    weight = total[2 * third_part :] + 1.0
     piece[...] = jnp.concatenate(
-        [total[:halves] / weight, total[halves : 2 * halves] / weight], axis=0
+        [total[:third_part] / weight, total[third_part : 2 * third_part] / weight], axis=0
     )
     third = [
         started(
@@ -571,7 +572,9 @@
     steps[row] = piece[...]
     for copy in third:
         copy.wait_recv()
-    joined[...] = jnp.concatenate([steps[index] for index in range(n_row)], axis=1)
+    for plane in range(comps):
+        rows = slice(plane * part, (plane + 1) * part)
+        joined[plane] = jnp.concatenate([steps[index, rows] for index in range(n_row)], axis=0)
     got_steps[col] = joined[...]
     count = n_col // 2
     place, core = col // 2, lax.rem(col, 2)
@@ -606,6 +609,7 @@
         relay_halos, finish_halos = send_halos(
             near, narrow, rims, halo_send, halo_recv, lambda: None
         )
+        leaving = local_copy(new_block, block_out, load.at[2])
 
     for step in range(1, count):
         across[step - 1].wait_recv()
@@ -627,6 +631,7 @@
         pl.when(piece_of[3])(copy.wait_send)
     if halos:
         finish_halos()
+        leaving.wait()
 
 
 def exchange(block, own_grad, grad_rims, sums, probe_field, halos):
@@ -635,6 +640,7 @@
     chunk = size // n_col
     part = chunk // n_row
     comps = planes * 2 // 3
+    padded = -(-planes * part // 16) * 16
     vmem = pl.BlockSpec(memory_space=pltpu.VMEM)
     hbm = pl.BlockSpec(memory_space=pl.ANY)
     dma = pltpu.SemaphoreType.DMA
@@ -647,19 +653,21 @@
             jax.ShapeDtypeStruct(probe_field.shape, jnp.float32),
             *fresh,
         ),
-        in_specs=[hbm] * 7,
-        out_specs=(vmem, vmem) + (hbm,) * len(fresh),
+        in_specs=[hbm, vmem, hbm, hbm, hbm, vmem, vmem],
+        out_specs=(pl.BlockSpec(memory_space=pltpu.HBM) if halos else vmem, vmem)
+        + (hbm,) * len(fresh),
         scratch_shapes=[
-            *[pltpu.VMEM(value.shape, jnp.float32) for value in (block, own_grad, sums, probe_field)],
-            dma((5,)),
+            *[pltpu.VMEM(block.shape, jnp.float32)] * (2 if halos else 1),
+            dma((3,)),
             *[pltpu.VMEM(shape.shape, shape.dtype) for shape in shapes],
             pltpu.VMEM(block.shape, jnp.bfloat16),
             pltpu.VMEM(sums.shape, jnp.bfloat16),
             pltpu.VMEM((n_col - 1, planes, chunk, LANES), jnp.bfloat16),
-            pltpu.VMEM((n_row, planes, part, LANES), jnp.float32),
-            pltpu.VMEM((n_row - 1, planes, part, LANES), jnp.float32),
-            pltpu.VMEM((comps, part, LANES), jnp.float32),
-            pltpu.VMEM((n_row, comps, part, LANES), jnp.float32),
+            pltpu.VMEM((n_row, planes * part, LANES), jnp.float32),
+            pltpu.VMEM((n_row, padded, LANES), jnp.bfloat16),
+            pltpu.VMEM((n_row - 1, padded, LANES), jnp.bfloat16),
+            pltpu.VMEM((comps * part, LANES), jnp.float32),
+            pltpu.VMEM((n_row, comps * part, LANES), jnp.float32),
             pltpu.VMEM((comps, chunk, LANES), jnp.float32),
             pltpu.VMEM((n_col, comps, chunk, LANES), jnp.float32),
             pltpu.VMEM(shapes[2].shape, shapes[2].dtype),

time: 116 us -> 113 us (0.974)
  Pallas kernels: 108 us -> 105 us
    pallas_call x2, Pallas kernels: 75.1 us -> 73.7 us  [exchange(): pl.pallas_call(functools.partial(exchange_kernel, n_row, n_col, halos), o...]
    pallas_call x2, Pallas kernels: 17.6 us -> 16.4 us  [frame_sums(): pl.pallas_call(functools.partial(frames_kernel, iteration), out_shape=(ja...]
where the time goes in v5:
time: 113 us; the launch traced here: 111 us
  Pallas kernels  105 us (93%)
  local copies, waits for them, and re-layouts  5.25 us (5%)
    pallas_call x2, Pallas kernels, exchange(): pl.pallas_call(functools.partial(exchange_kernel, n_row, n_col, halos), o...  73.7 us
    pallas_call x2, Pallas kernels, frame_sums(): pl.pallas_call(functools.partial(frames_kernel, iteration), out_shape=(ja...  16.4 us
    pallas_call x1, Pallas kernels, first_halos(): pl.pallas_call(functools.partial(halo_kernel, n_row, n_col), out_shape=ri...  15.2 us
    unnamed x17, local copies, waits for them, and re-layouts  5.25 us

profile of v5, /device:TPU:25, one launch (start us, length us, event | category | flops | bytes accessed | tf_op | source)
XLA Modules:
  0.0 111.3 jit_solution(2192244718360415485)
XLA Ops:
  0.6 0.0 copy-start.4
  0.6 0.7 copy.9.live
  1.4 0.0 copy-start
  1.4 1.4 %copy-done = f32[2,512,384]{2,1,0:T(8,128)S(1)} copy-done((f32[2,512,384]{2,1,0:T(8,128)S(1)}, f32[2,512,384]{2,1,0:T(8,128)}, u32[]{:S(2)}) %copy-start) | copy-done | bytes 1572888
  2.8 0.0 copy-start.3
  2.8 0.0 copy-start.5
  2.8 0.0 copy-start.6
  2.8 15.2 %first_halos.1 = (bf16[2,256,384]{2,1,0:T(8,128)(2,1)S(1)}, bf16[2,512,256]{2,1,0:T(8,128)(2,1)S(1)}, bf16[2,256,256]{2,1,0:T(8,128)(2,1)S(1)}) custom-call(f32[2,512,384]{2,1,0:T(8,128)S(1)} %copy-done), custom_call_target="tpu_custom_call" | custom-call | flops 393216 | bytes 4194304 | tf_op jit(solution)/shard_map/first_halos/pallas_call | solution.py:383
  18.0 0.0 copy-done.4
  18.0 0.0 copy-done.3
  18.0 0.0 copy-done.5
  18.1 0.0 copy-done.6
  18.1 8.2 %frames.2 = (f32[2,64,8,384]{3,2,1,0:T(8,128)}, bf16[2,256,384]{2,1,0:T(8,128)(2,1)S(1)}, bf16[2,512,256]{2,1,0:T(8,128)(2,1)S(1)}, bf16[2,256,256]{2,1,0:T(8,128)(2,1)S(1)}, f32[6,256,128]{2,1,0:T(8,128)S(1)}) custom-call(s32[2,2,12]{2,1,0:T(2,128)S(1)} %copy-done.4, s32[2,1,1]{2,1,0:T(1,128)S(1)} %copy.9.live, f32[2,64,8,384]{3,2,1,0:T(8,128)} %bitcast.4, ...), custom_call_target="tpu_custom_call" | custom-call | flops 6442450944 | bytes 12582912 | tf_op jit(solution)/shard_map/frames/pallas_call | solution.py:243
  26.3 40.9 %exchange.2 = (f32[2,512,384]{2,1,0:T(8,128)S(1)}, f32[2,256,256]{2,1,0:T(8,128)S(1)}, bf16[2,256,384]{2,1,0:T(8,128)(2,1)S(1)}, bf16[2,512,256]{2,1,0:T(8,128)(2,1)S(1)}, bf16[2,256,256]{2,1,0:T(8,128)(2,1)S(1)}) custom-call(f32[2,512,384]{2,1,0:T(8,128)} %refs_0_.1, f32[2,512,384]{2,1,0:T(8,128)} %bitcast.7, ...), custom_call_target="tpu_custom_call" | custom-call | flops 786432 | bytes 8388608 | tf_op jit(solution)/shard_map/exchange/pallas_call | solution.py:649
  67.2 0.0 copy-start.1
  67.2 1.1 %copy-done.1 = f32[2,512,384]{2,1,0:T(8,128)} copy-done((f32[2,512,384]{2,1,0:T(8,128)}, f32[2,512,384]{2,1,0:T(8,128)S(1)}, u32[]{:S(2)}) %copy-start.1) | copy-done | bytes 1572888
  68.3 0.0 copy-start.2
  68.3 8.2 %frames.3 = (f32[2,64,8,384]{3,2,1,0:T(8,128)}, bf16[2,256,384]{2,1,0:T(8,128)(2,1)S(1)}, bf16[2,512,256]{2,1,0:T(8,128)(2,1)S(1)}, bf16[2,256,256]{2,1,0:T(8,128)(2,1)S(1)}, f32[6,256,128]{2,1,0:T(8,128)S(1)}) custom-call(s32[2,2,12]{2,1,0:T(2,128)S(1)} %copy-done.4, s32[2,1,1]{2,1,0:T(1,128)S(1)} %copy.9.live, f32[2,64,8,384]{3,2,1,0:T(8,128)} %bitcast.5, ...), custom_call_target="tpu_custom_call" | custom-call | flops 6442450944 | bytes 12582912 | tf_op jit(solution)/shard_map/frames/pallas_call | solution.py:243
  76.6 0.0 copy-done.2
  76.6 32.8 %exchange.3 = (f32[2,512,384]{2,1,0:T(8,128)S(1)}, f32[2,256,256]{2,1,0:T(8,128)S(1)}) custom-call(f32[2,512,384]{2,1,0:T(8,128)S(1)} %copy-done.2, f32[2,512,384]{2,1,0:T(8,128)} %bitcast.6, bf16[2,256,384]{2,1,0:T(8,128)(2,1)S(1)} %get-tuple-element.34.refs_2_, bf16[2,512,256]{2,1,0:T(8,128)(2,1)S(1)} %get-tuple-element.35.refs_3_, ...), custom_call_target="tpu_custom_call" | custom-call | flops 786432 | bytes 8388608 | tf_op jit(solution)/shard_map/exchange/pallas_call | solution.py:649
  109.4 1.1 %copy.13 = f32[2,512,384]{2,1,0:T(8,128)} copy(f32[2,512,384]{2,1,0:T(8,128)S(1)} %get-tuple-element.40) | data formatting | bytes 3145728
  110.5 0.8 copy.14
Async XLA Ops:
  0.6 17.4 %copy-start.4 = (s32[2,2,12]{2,1,0:T(2,128)S(1)}, s32[2,2,12]{2,1,0:T(2,128)}, u32[]{:S(2)}) copy-start(s32[2,2,12]{2,1,0:T(2,128)} %positions.3) | copy-start | bytes 580
  1.4 1.4 %copy-start = (f32[2,512,384]{2,1,0:T(8,128)S(1)}, f32[2,512,384]{2,1,0:T(8,128)}, u32[]{:S(2)}) copy-start(f32[2,512,384]{2,1,0:T(8,128)} %refs_0_.1) | copy-start | bytes 4718596
  2.8 15.2 %copy-start.3 = (f32[2,256,256]{2,1,0:T(8,128)S(1)}, f32[2,256,256]{2,1,0:T(8,128)}, u32[]{:S(2)}) copy-start(f32[2,256,256]{2,1,0:T(8,128)} %refs_6_.1) | copy-start | bytes 1572868
  2.8 15.3 %copy-start.5 = (bf16[512,512]{1,0:T(8,128)(2,1)S(1)}, bf16[512,512]{1,0:T(8,128)(2,1)}, u32[]{:S(2)}) copy-start(bf16[512,512]{1,0:T(8,128)(2,1)} %constant.5.clone.right_hbm) | copy-start | bytes 1572868
  2.8 15.3 %copy-start.6 = (bf16[512,512]{1,0:T(8,128)(2,1)S(1)}, bf16[512,512]{1,0:T(8,128)(2,1)}, u32[]{:S(2)}) copy-start(bf16[512,512]{1,0:T(8,128)(2,1)} %constant.4.clone.left_hbm) | copy-start | bytes 1572868
  67.2 1.1 %copy-start.1 = (f32[2,512,384]{2,1,0:T(8,128)}, f32[2,512,384]{2,1,0:T(8,128)S(1)}, u32[]{:S(2)}) copy-start(f32[2,512,384]{2,1,0:T(8,128)S(1)} %get-tuple-element.28.refs_0_) | copy-start | bytes 4718596
  68.3 8.2 %copy-start.2 = (f32[2,512,384]{2,1,0:T(8,128)S(1)}, f32[2,512,384]{2,1,0:T(8,128)}, u32[]{:S(2)}) copy-start(f32[2,512,384]{2,1,0:T(8,128)} %copy-done.1) | copy-start | bytes 4718596
